TPU v7x, 32 devices: a whole 2x2x4 slice. The times are simulated.
32 devices in a mesh: groups: 2 (over x), seq: 16 (over z, y, core).
Axes of the slice: x: 2, y: 2, z: 4, core: 2. Of those that a mesh axis runs over, the one named last changes fastest.
Arguments:
- out_grad: bfloat16 [2048, 4096], P(None, ('groups', 'seq')), parts along dimension 1, may hold values from -6 to 6
- gate_one: bfloat16 [2048, 4096], P(None, ('groups', 'seq')), parts along dimension 1, may hold values from -6 to 6
- gate_two: bfloat16 [2048, 4096], P(None, ('groups', 'seq')), parts along dimension 1, may hold values from -6 to 6
- conv_one: bfloat16 [2048, 4096], P(None, ('groups', 'seq')), parts along dimension 1, may hold values from -6 to 6
- conv_two: bfloat16 [2048, 4096], P(None, ('groups', 'seq')), parts along dimension 1, may hold values from -6 to 6
- value: bfloat16 [2048, 4096], P(None, ('groups', 'seq')), parts along dimension 1, may hold values from -6 to 6
- filter_one: float32 [2048, 2048], P('seq'), may hold values from -6 to 6
- filter_two: float32 [2048, 2048], P('seq'), may hold values from -6 to 6
- skip_one: float32 [2048], P('seq'), may hold values from -4 to 4
- skip_two: float32 [2048], P('seq'), may hold values from -4 to 4
- short_weight: float32 [2048, 3], replicated, may hold values from -3.5 to 3.5
Outputs:
- proj_grad: bfloat16 [2048, 4096], P(None, ('groups', 'seq')), parts along dimension 1
- gate_one_grad: bfloat16 [2048, 4096], P(None, ('groups', 'seq')), parts along dimension 1
- gate_two_grad: bfloat16 [2048, 4096], P(None, ('groups', 'seq')), parts along dimension 1
- filter_one_grad: float32 [4096, 2048], P(('groups', 'seq')), parts along dimension 0
- filter_two_grad: float32 [4096, 2048], P(('groups', 'seq')), parts along dimension 0
There are 2 independent parts, one for each index of `groups`. A program takes and returns all parts, laid end to end along the dimension named above; an argument that names none is the same for every part. Nothing has to cross between parts.
All inputs are finite; a program needn't handle non-finite values.
Results may differ from a plain program's by a relative error of at most 0.0025.
Values may be sent and summed in bfloat16 or wider, within the bound.
No kernel may reach another device: no remote copies, remote signals or barrier semaphores. Data moves between devices by JAX's collectives and lax.ppermute only.
A program may use at most 128 MiB of HBM per device.

v0:
```python
import functools
import math

import jax
import jax.numpy as jnp
import numpy as np
from jax import lax
from jax.experimental import pallas as pl
from jax.experimental.pallas import tpu as pltpu
from jax.sharding import PartitionSpec as P

F32 = jnp.float32
BF16 = jnp.bfloat16
ROWS = 16


def cmul_const(x, angle, gain=1.0):
    re, im = x
    c, s = gain * math.cos(angle), gain * math.sin(angle)
    if abs(s) < 1e-12:
        if abs(c - 1.0) < 1e-12:
            return x
        return (re * c, im * c)
    if abs(c) < 1e-12:
        if abs(s + 1.0) < 1e-12:
            return (im, -re)
        if abs(s - 1.0) < 1e-12:
            return (-im, re)
    if abs(abs(c) - abs(s)) < 1e-12:
        m = abs(c)
        sc, ss = (1.0 if c > 0 else -1.0), (1.0 if s > 0 else -1.0)
        a = (re - im) if sc * ss > 0 else (re + im)
        b = (re + im) if sc * ss > 0 else (im - re)
        return (a * (m * sc), b * (m * sc))
    return (re * c - im * s, re * s + im * c)


def cdft(xs, sign):
    n = len(xs)
    if n == 1:
        return list(xs)
    even, odd = cdft(xs[0::2], sign), cdft(xs[1::2], sign)
    half = n // 2
    low, high = [], []
    for k in range(half):
        (er, ei), (tr, ti) = even[k], cmul_const(odd[k], sign * 2.0 * math.pi * k / n)
        low.append((er + tr, ei + ti))
        high.append((er - tr, ei - ti))
    return low + high


def odd_part(y, n):
    quarter = n // 4
    u = [cmul_const((y[j], -y[j + quarter]), -2.0 * math.pi * j / n) for j in range(quarter)]
    out = {}
    for p, (re, im) in enumerate(cdft(u, -1)):
        k = 4 * p + 1
        if k <= n // 2:
            out[k] = (re, im)
        else:
            out[n - k] = (re, -im)
    return out


def rdft(xs):
    n = len(xs)
    if n == 1:
        return [(xs[0], None)]
    half = n // 2
    even = rdft([xs[j] + xs[j + half] for j in range(half)])
    if n == 2:
        return [even[0], (xs[0] - xs[1], None)]
    odd = odd_part([xs[j] - xs[j + half] for j in range(half)], n)
    return [even[k // 2] if k % 2 == 0 else odd[k] for k in range(half + 1)]


def rdft_padded(xs):
    n = 2 * len(xs)
    even, odd = rdft(xs), odd_part(xs, n)
    return [even[k // 2] if k % 2 == 0 else odd[k] for k in range(len(xs) + 1)]


def odd_back(spec, n):
    quarter = n // 4
    u = []
    for p in range(quarter):
        k = 4 * p + 1
        if k <= n // 2:
            u.append(spec[k])
        else:
            re, im = spec[n - k]
            u.append((re, -im))
    v = cdft(u, 1)
    low, high = [], []
    for j in range(quarter):
        re, im = cmul_const(v[j], 2.0 * math.pi * j / n, 2.0)
        low.append(re)
        high.append(-im)
    return low + high


def irdft(spec):
    n = 2 * (len(spec) - 1)
    if n == 2:
        a, b = spec[0][0], spec[1][0]
        return [a + b, a - b]
    even, odd = irdft(spec[0::2]), odd_back(spec, n)
    return [e + o for e, o in zip(even, odd)] + [e - o for e, o in zip(even, odd)]


def irdft_half(spec):
    n = 2 * (len(spec) - 1)
    even, odd = irdft(spec[0::2]), odd_back(spec, n)
    return [e + o for e, o in zip(even, odd)]


def split(x):
    hi = x.astype(BF16)
    return hi, (x - hi.astype(F32)).astype(BF16)


def tables(blocks, width, scale):
    k1 = np.arange(blocks + 1, dtype=np.float64)[:, None]
    f = np.arange(width, dtype=np.float64)
    total = 2 * blocks * width
    angle = 2.0 * np.pi * (k1 * f[None, :]) / total
    twiddle = np.stack([np.cos(angle), -np.sin(angle)], axis=1).reshape(-1, width)
    theta = 2.0 * np.pi * ((f[:, None] * f[None, :]) % width) / width
    c, s = np.cos(theta), np.sin(theta)
    matrix = np.block([[c, -s], [s, c]]).astype(np.float32)
    hi = matrix.astype(jnp.bfloat16)
    lo = (matrix - hi.astype(np.float32)).astype(jnp.bfloat16)
    return hi, lo, twiddle.astype(np.float32), (twiddle * scale).astype(np.float32)


def row_tile(rows):
    best = ROWS
    for size in range(ROWS, 289, ROWS):
        if rows % size == 0:
            best = size
    return best


def spread(read, twiddle_ref, hi_ref, lo_ref, channels, blocks, width):
    def body(g, carry):
        start = pl.multiple_of(g * ROWS, ROWS)
        spec = rdft_padded([read(b, start) for b in range(blocks)])
        for k, (re, im) in enumerate(spec):
            c = twiddle_ref[2 * k : 2 * k + 1, :]
            s = twiddle_ref[2 * k + 1 : 2 * k + 2, :]
            if im is None:
                tr, ti = re * c, re * s
            else:
                tr, ti = re * c - im * s, re * s + im * c
            rows = pl.ds(pl.multiple_of(k * channels + start, ROWS), ROWS)
            for value, at in ((tr, 0), (ti, width)):
                hi, lo = split(value)
                hi_ref[rows, at : at + width] = hi
                lo_ref[rows, at : at + width] = lo
        return carry

    lax.fori_loop(0, channels // ROWS, body, 0)


def gather(spec_ref, twiddle_ref, start, channels, blocks, width):
    spec = []
    for k in range(blocks + 1):
        rows = pl.ds(pl.multiple_of(k * channels + start, ROWS), ROWS)
        re, im = spec_ref[rows, :width], spec_ref[rows, width:]
        c = twiddle_ref[2 * k : 2 * k + 1, :]
        s = twiddle_ref[2 * k + 1 : 2 * k + 2, :]
        if k == 0 or k == blocks:
            spec.append((re * c + im * s, None))
        else:
            spec.append((re * c + im * s, im * c - re * s))
    return irdft_half(spec)


def dot3(hi, lo, mat_hi, mat_lo, dims):
    def dot(a, b):
        return lax.dot_general(a, b, (dims, ((), ())), preferred_element_type=F32)

    return dot(hi, mat_hi) + dot(lo, mat_hi) + dot(hi, mat_lo)


FORWARD = ((1,), (0,))
BACK = ((1,), (1,))


def spectrum_kernel(channels, blocks, width, one_ref, two_ref, mat_hi, mat_lo, tw_ref,
                    out_one, out_two, hi_ref, lo_ref):
    rows = (blocks + 1) * channels
    tile = row_tile(rows)
    for filt, out in ((two_ref, out_two), (one_ref, out_one)):
        spread(lambda b, start: filt[pl.ds(start, ROWS), b * width : (b + 1) * width],
               tw_ref, hi_ref, lo_ref, channels, blocks, width)
        for at in range(0, rows, tile):
            out[at : at + tile, :] = dot3(
                hi_ref[at : at + tile, :], lo_ref[at : at + tile, :],
                mat_hi[...], mat_lo[...], FORWARD)


def multiply_back(spec, other, mat_hi, mat_lo, width):
    gr, gi = spec[:, :width], spec[:, width:]
    hr, hi = other[:, :width], other[:, width:]
    zr, zi = gr * hr + gi * hi, gi * hr - gr * hi
    z_hi, z_lo = split(jnp.concatenate([zr, zi], axis=1))
    return dot3(z_hi, z_lo, mat_hi[...], mat_lo[...], BACK)


def adjoint_kernel(channels, blocks, width, in_ref, h_two, h_one, skip_two, skip_one, taps_ref,
                   mat_hi, mat_lo, tw_ref, out_ref, spec_two, spec_one, hi_ref, lo_ref, back_ref,
                   grad_ref):
    rows = (blocks + 1) * channels
    tile = row_tile(rows)

    def convolve(h_ref, spec_ref):
        for at in range(0, rows, tile):
            here = slice(at, at + tile)
            spec = dot3(hi_ref[here, :], lo_ref[here, :], mat_hi[...], mat_lo[...], FORWARD)
            spec_ref[here, :] = spec
            back_ref[here, :] = multiply_back(spec, h_ref[here, :], mat_hi, mat_lo, width)

    spread(lambda b, start: in_ref[b, 0, pl.ds(start, ROWS), :].astype(F32),
           tw_ref, hi_ref, lo_ref, channels, blocks, width)
    convolve(h_two, spec_two)

    def first(g, carry):
        start = pl.multiple_of(g * ROWS, ROWS)
        here = pl.ds(start, ROWS)
        skip = skip_two[here, :]
        back = gather(back_ref, tw_ref, start, channels, blocks, width)
        for b in range(blocks):
            full = back[b] + skip * in_ref[b, 0, here, :].astype(F32)
            grad = full.astype(BF16)
            out_ref[b, 0, here, :] = grad
            grad_ref[b, here, :] = (grad.astype(F32) * in_ref[b, 1, here, :].astype(F32)).astype(BF16)
        return carry

    lax.fori_loop(0, channels // ROWS, first, 0)
    spread(lambda b, start: grad_ref[b, pl.ds(start, ROWS), :].astype(F32),
           tw_ref, hi_ref, lo_ref, channels, blocks, width)
    convolve(h_one, spec_one)
    lane = lax.broadcasted_iota(jnp.int32, (ROWS, width), 1)
    count = taps_ref.shape[1]

    def second(g, carry):
        start = pl.multiple_of(g * ROWS, ROWS)
        here = pl.ds(start, ROWS)
        skip = skip_one[here, :]
        back = gather(back_ref, tw_ref, start, channels, blocks, width)
        grads = []
        for b in range(blocks):
            full = back[b] + skip * grad_ref[b, here, :].astype(F32)
            grads.append(full.astype(BF16).astype(F32))
        grads.append(jnp.zeros((ROWS, width), F32))
        sums = [taps_ref[here, 0:1] * grads[b] for b in range(blocks)]
        for k in range(1, count):
            turned = [pltpu.roll(v, width - k, 1) for v in grads]
            for b in range(blocks):
                moved = jnp.where(lane < width - k, turned[b], turned[b + 1])
                sums[b] = sums[b] + taps_ref[here, k : k + 1] * moved
        for b in range(blocks):
            out_ref[b, 1, here, :] = sums[b].astype(BF16)
        return carry

    lax.fori_loop(0, channels // ROWS, second, 0)


def filter_kernel(channels, blocks, width, in_ref, spec_two, spec_one, mat_hi, mat_lo, tw_ref,
                  tw_scaled, out_one, out_two, hi_ref, lo_ref, back_ref):
    rows = (blocks + 1) * channels
    tile = row_tile(rows)
    for index, spec_ref, out in ((0, spec_two, out_two), (1, spec_one, out_one)):
        spread(lambda b, start: in_ref[b, index, pl.ds(start, ROWS), :].astype(F32),
               tw_scaled, hi_ref, lo_ref, channels, blocks, width)
        for at in range(0, rows, tile):
            here = slice(at, at + tile)
            other = dot3(hi_ref[here, :], lo_ref[here, :], mat_hi[...], mat_lo[...], FORWARD)
            back_ref[here, :] = multiply_back(spec_ref[here, :], other, mat_hi, mat_lo, width)

        def body(g, carry):
            start = pl.multiple_of(g * ROWS, ROWS)
            back = gather(back_ref, tw_ref, start, channels, blocks, width)
            for b in range(blocks):
                out[pl.ds(start, ROWS), b * width : (b + 1) * width] = back[b]
            return carry

        lax.fori_loop(0, channels // ROWS, body, 0)


def call(kernel, out_shape, scratch, flops, moved, *args):
    vmem = pl.BlockSpec(memory_space=pltpu.VMEM)
    return pl.pallas_call(
        kernel,
        out_shape=out_shape,
        in_specs=[vmem] * len(args),
        out_specs=[vmem] * len(out_shape),
        scratch_shapes=scratch,
        compiler_params=pltpu.CompilerParams(vmem_limit_bytes=44 * 1024 * 1024),
        cost_estimate=pl.CostEstimate(flops=flops, bytes_accessed=moved, transcendentals=0),
    )(*args)


def exchange(value):
    return lax.all_to_all(value, "seq", split_axis=0, concat_axis=0, tiled=True)


def local(
    out_grad,
    gate_one,
    gate_two,
    conv_one,
    conv_two,
    value,
    filter_one,
    filter_two,
    skip_one,
    skip_two,
    short_weight,
):
    blocks = lax.axis_size("seq")
    width = out_grad.shape[1]
    channels = filter_one.shape[0]
    length = filter_one.shape[1]
    rows = (blocks + 1) * channels
    shape = (blocks, channels, width)
    mat_hi, mat_lo, tw, tw_scaled = tables(
        blocks, width, length ** (-0.5) / (2 * length))
    work = 3 * 2 * rows * (2 * width) ** 2
    size = rows * 2 * width * 4

    def struct(*dims, dtype=F32):
        return jax.ShapeDtypeStruct(dims, dtype)

    def product(a, b):
        return (a.astype(F32) * b.astype(F32)).astype(BF16)

    halves = [pltpu.VMEM((rows, 2 * width), BF16), pltpu.VMEM((rows, 2 * width), BF16)]
    back = pltpu.VMEM((rows, 2 * width), F32)
    spec = struct(rows, 2 * width)

    cg_two = product(out_grad, gate_two).reshape(shape)
    first = exchange(jnp.stack([cg_two, gate_one.reshape(shape)], axis=1))
    inner = product(gate_one, conv_one).reshape(shape)
    second_in = jnp.stack([inner, value.reshape(shape)], axis=1)

    h_one, h_two = call(
        functools.partial(spectrum_kernel, channels, blocks, width),
        [spec, spec], halves, 2 * work, 4 * size,
        filter_one, filter_two, mat_hi, mat_lo, tw_scaled)
    second_in, first = lax.optimization_barrier((second_in, first))
    second = exchange(second_in)

    me = lax.axis_index("seq")
    taps = lax.dynamic_slice_in_dim(short_weight, me * channels, channels, axis=0)
    grads, spec_two, spec_one = call(
        functools.partial(adjoint_kernel, channels, blocks, width),
        [struct(blocks, 2, channels, width, dtype=BF16), spec, spec],
        halves + [back, pltpu.VMEM(shape, BF16)], 4 * work, 8 * size,
        first, h_two, h_one, skip_two[:, None], skip_one[:, None], taps, mat_hi, mat_lo, tw)
    grads, second = lax.optimization_barrier((grads, second))
    third = exchange(grads)

    filter_one_grad, filter_two_grad = call(
        functools.partial(filter_kernel, channels, blocks, width),
        [struct(channels, length), struct(channels, length)],
        halves + [back], 4 * work, 8 * size,
        second, spec_two, spec_one, mat_hi, mat_lo, tw, tw_scaled)
    gate_two_grad = product(out_grad, conv_two)
    inner_grad = third[:, 0].reshape(out_grad.shape)
    proj_grad = third[:, 1].reshape(out_grad.shape)
    gate_one_grad = product(inner_grad, conv_one)
    return (proj_grad, gate_one_grad, gate_two_grad, filter_one_grad, filter_two_grad)


def solution(mesh):
    frames = P(None, ("groups", "seq"))
    return jax.shard_map(
        local,
        mesh=mesh,
        in_specs=(frames,) * 6 + (P("seq", None),) * 2 + (P("seq"),) * 2 + (P(),),
        out_specs=(frames,) * 3 + (P(("groups", "seq"), None),) * 2,
        check_vma=False,
    )
```

profile of v0, /device:TPU:9, one launch (start us, length us, event | category | flops | bytes accessed | tf_op | source)
XLA Modules:
  0.0 97.1 jit_solution(9959250194274326209)
XLA Ops:
  0.7 2.4 %fusion.3 = (bf16[2048,128]{1,0:T(8,128)(2,1)}, bf16[2048,128]{1,0:T(8,128)(2,1)S(1)}) fusion(bf16[2048,128]{1,0:T(8,128)(2,1)} %param.15, bf16[2048,128]{1,0:T(8,128)(2,1)} %param.19, bf16[2048,128]{1,0:T(8,128)(2,1)} %param.17), kind=kLoop, calls=%fused_computation.7 | loop fusion | flops 1835008 | bytes 2621440 | tf_op jit(solution)/shard_map/convert_element_type | solution.py:337
  3.1 1.1 %pad_maximum_fusion.1 = bf16[16,2,128,128]{3,2,1,0:T(8,128)(2,1)} fusion(bf16[16,1,128,128]{3,2,1,0:T(8,128)(2,1)S(1)} %bitcast.10, bf16[16,1,128,128]{3,2,1,0:T(8,128)(2,1)S(1)} %bitcast.11), kind=kLoop, calls=%fused_computation.9 | loop fusion | flops 524288 | bytes 2097152 | tf_op jit(solution)/shard_map/stack | solution.py:344
  4.2 6.6 %all-to-all-start = ((bf16[16,2,128,128]{3,2,1,0:T(8,128)(2,1)}), bf16[16,2,128,128]{3,2,1,0:T(8,128)(2,1)S(1)}, u32[]{:S(2)}, u32[]{:S(2)}) async-start(bf16[16,2,128,128]{3,2,1,0:T(8,128)(2,1)} %pad_maximum_fusion.1), calls=%async_computation | async-start | bytes 2097152 | tf_op jit(solution)/shard_map/all_to_all | solution.py:306
  10.8 0.1 fusion
  11.0 2.2 %pad_maximum_fusion = bf16[16,2,128,128]{3,2,1,0:T(8,128)(2,1)} fusion(bf16[16,1,128,128]{3,2,1,0:T(8,128)(2,1)} %bitcast.13, bf16[16,1,128,128]{3,2,1,0:T(8,128)(2,1)S(1)} %bitcast.12), kind=kLoop, calls=%fused_computation.8 | loop fusion | flops 524288 | bytes 2097152 | tf_op jit(solution)/shard_map/stack | solution.py:346
  13.2 22.4 %all-to-all-done.in_ref = bf16[16,2,128,128]{3,2,1,0:T(8,128)(2,1)S(1)} async-done(((bf16[16,2,128,128]{3,2,1,0:T(8,128)(2,1)}), bf16[16,2,128,128]{3,2,1,0:T(8,128)(2,1)S(1)}, u32[]{:S(2)}, u32[]{:S(2)}) %all-to-all-start) | async-done | bytes 1048608 | tf_op jit(solution)/shard_map/all_to_all | solution.py:306
  35.6 5.0 %all-to-all-start.1 = ((bf16[16,2,128,128]{3,2,1,0:T(8,128)(2,1)}), bf16[16,2,128,128]{3,2,1,0:T(8,128)(2,1)S(1)}, u32[]{:S(2)}, u32[]{:S(2)}) async-start(bf16[16,2,128,128]{3,2,1,0:T(8,128)(2,1)} %pad_maximum_fusion), calls=%async_computation.1 | async-start | bytes 2097152 | tf_op jit(solution)/shard_map/all_to_all | solution.py:306
  40.7 0.1 copy.22.skip_one
  40.9 0.1 copy.21.skip_two
  41.0 1.2 %copy-done.2 = f32[128,2048]{1,0:T(8,128)S(1)} copy-done((f32[128,2048]{1,0:T(8,128)S(1)}, f32[128,2048]{1,0:T(8,128)}, u32[]{:S(2)}) %copy-start.2) | copy-done | bytes 1048600
  42.2 0.9 copy-done.4
  43.1 4.4 %shard_map.182 = (f32[2176,256]{1,0:T(8,128)S(1)}, f32[2176,256]{1,0:T(8,128)S(1)}) custom-call(f32[128,2048]{1,0:T(8,128)S(1)} %copy-done.1, f32[128,2048]{1,0:T(8,128)S(1)} %copy-done.2, bf16[256,256]{1,0:T(8,128)(2,1)S(1)} %copy-done.4, bf16[256,256]{1,0:T(8,128)(2,1)S(1)} %copy-done.3, f32[34,128]{1,0:T(8,128)S(1)} %copy-done.7), custom_call_target="tpu_custom_call" | custom-call | flops 1711276032 | bytes 8912896 | tf_op jit(solution)/shard_map/pallas_call | solution.py:294
  47.5 1.4 %copy-done.9 = f32[2176,256]{1,0:T(8,128)} copy-done((f32[2176,256]{1,0:T(8,128)}, f32[2176,256]{1,0:T(8,128)S(1)}, u32[]{:S(2)}) %copy-start.9) | copy-done | bytes 2228248
  48.9 12.3 %shard_map.183 = (bf16[16,2,128,128]{3,2,1,0:T(8,128)(2,1)}, f32[2176,256]{1,0:T(8,128)S(1)}, f32[2176,256]{1,0:T(8,128)S(1)}) custom-call(bf16[16,2,128,128]{3,2,1,0:T(8,128)(2,1)S(1)} %all-to-all-done.in_ref, f32[2176,256]{1,0:T(8,128)S(1)} %get-tuple-element.17.h_two, f32[2176,256]{1,0:T(8,128)} %copy-done.9, f32[128,1]{1,0:T(8,128)S(1)} %copy.21.skip_two, ...), custom_call_target="tpu_custom_call" | custom-call | flops 3422552064 | bytes 17825792 | tf_op jit(solution)/shard_map/pallas_call | solution.py:294
  61.3 1.4 %copy-done.10 = f32[2176,256]{1,0:T(8,128)} copy-done((f32[2176,256]{1,0:T(8,128)}, f32[2176,256]{1,0:T(8,128)S(1)}, u32[]{:S(2)}) %copy-start.10) | copy-done | bytes 2228248
  62.7 1.4 %copy-done.12 = f32[2176,256]{1,0:T(8,128)} copy-done((f32[2176,256]{1,0:T(8,128)}, f32[2176,256]{1,0:T(8,128)S(1)}, u32[]{:S(2)}) %copy-start.12) | copy-done | bytes 2228248
  64.0 1.4 %all-to-all-done.1.in_ref = bf16[16,2,128,128]{3,2,1,0:T(8,128)(2,1)S(1)} async-done(((bf16[16,2,128,128]{3,2,1,0:T(8,128)(2,1)}), bf16[16,2,128,128]{3,2,1,0:T(8,128)(2,1)S(1)}, u32[]{:S(2)}, u32[]{:S(2)}) %all-to-all-start.1) | async-done | bytes 1048608 | tf_op jit(solution)/shard_map/all_to_all | solution.py:306
  65.4 5.0 %all-to-all-start.2 = ((bf16[16,2,128,128]{3,2,1,0:T(8,128)(2,1)}), bf16[16,2,128,128]{3,2,1,0:T(8,128)(2,1)S(1)}, u32[]{:S(2)}, u32[]{:S(2)}) async-start(bf16[16,2,128,128]{3,2,1,0:T(8,128)(2,1)} %get-tuple-element.21), calls=%async_computation.2 | async-start | bytes 2097152 | tf_op jit(solution)/shard_map/all_to_all | solution.py:306
  70.4 1.6 %copy-done.11 = f32[2176,256]{1,0:T(8,128)S(1)} copy-done((f32[2176,256]{1,0:T(8,128)S(1)}, f32[2176,256]{1,0:T(8,128)}, u32[]{:S(2)}) %copy-start.11) | copy-done | bytes 2228248
  72.1 1.6 %copy-done.13 = f32[2176,256]{1,0:T(8,128)S(1)} copy-done((f32[2176,256]{1,0:T(8,128)S(1)}, f32[2176,256]{1,0:T(8,128)}, u32[]{:S(2)}) %copy-start.13) | copy-done | bytes 2228248
  73.7 9.7 %shard_map.184 = (f32[128,2048]{1,0:T(8,128)}, f32[128,2048]{1,0:T(8,128)}) custom-call(bf16[16,2,128,128]{3,2,1,0:T(8,128)(2,1)S(1)} %all-to-all-done.1.in_ref, f32[2176,256]{1,0:T(8,128)S(1)} %copy-done.11, f32[2176,256]{1,0:T(8,128)S(1)} %copy-done.13, bf16[256,256]{1,0:T(8,128)(2,1)S(1)} %copy-done.6, bf16[256,256]{1,0:T(8,128)(2,1)S(1)} %copy-done.3, ...), custom_call_target="tpu_custom_call" | custom-call | flops 3422552064 | bytes 17825792 | tf_op jit(solution)/shard_map/pallas_call | solution.py:294
  83.3 11.9 %all-to-all-done.2 = bf16[16,2,128,128]{3,2,1,0:T(8,128)(2,1)S(1)} async-done(((bf16[16,2,128,128]{3,2,1,0:T(8,128)(2,1)}), bf16[16,2,128,128]{3,2,1,0:T(8,128)(2,1)S(1)}, u32[]{:S(2)}, u32[]{:S(2)}) %all-to-all-start.2) | async-done | bytes 1048608 | tf_op jit(solution)/shard_map/all_to_all | solution.py:306
  95.3 0.9 fusion.4
  96.1 1.0 fusion.1
  (33 shorter events, 0.2 us)
Async XLA Ops:
  0.6 40.0 %copy-start = (f32[2048,3]{0,1:T(4,128)S(1)}, f32[2048,3]{0,1:T(4,128)}, u32[]{:S(2)}) copy-start(f32[2048,3]{0,1:T(4,128)} %param.25) | copy-start | bytes 73732
  0.6 2.5 %copy-start.16 = (bf16[2048,128]{1,0:T(8,128)(2,1)S(1)}, bf16[2048,128]{1,0:T(8,128)(2,1)}, u32[]{:S(2)}) copy-start(bf16[2048,128]{1,0:T(8,128)(2,1)} %param.16) | copy-start | bytes 1572868
  3.1 7.7 %copy-start.14 = (bf16[2048,128]{1,0:T(8,128)(2,1)S(1)}, bf16[2048,128]{1,0:T(8,128)(2,1)}, u32[]{:S(2)}) copy-start(bf16[2048,128]{1,0:T(8,128)(2,1)} %param.18) | copy-start | bytes 1572868
  4.2 31.5 %all-to-all-start = ((bf16[16,2,128,128]{3,2,1,0:T(8,128)(2,1)}), bf16[16,2,128,128]{3,2,1,0:T(8,128)(2,1)S(1)}, u32[]{:S(2)}, u32[]{:S(2)}) async-start(bf16[16,2,128,128]{3,2,1,0:T(8,128)(2,1)} %pad_maximum_fusion.1), calls=%async_computation | async-start | bytes 2097152 | tf_op jit(solution)/shard_map/all_to_all | solution.py:306
  10.9 29.8 %copy-start.17 = (f32[128]{0:T(128)S(1)}, f32[128]{0:T(128)}, u32[]{:S(2)}) copy-start(f32[128]{0:T(128)} %param.23) | copy-start | bytes 1540
  11.0 29.9 %copy-start.18 = (f32[128]{0:T(128)S(1)}, f32[128]{0:T(128)}, u32[]{:S(2)}) copy-start(f32[128]{0:T(128)} %param.24) | copy-start | bytes 1540
  11.0 30.0 %copy-start.1 = (f32[128,2048]{1,0:T(8,128)S(1)}, f32[128,2048]{1,0:T(8,128)}, u32[]{:S(2)}) copy-start(f32[128,2048]{1,0:T(8,128)} %one_ref.1) | copy-start | bytes 3145732
  11.0 30.0 %copy-start.3 = (bf16[256,256]{1,0:T(8,128)(2,1)S(1)}, bf16[256,256]{1,0:T(8,128)(2,1)}, u32[]{:S(2)}) copy-start(bf16[256,256]{1,0:T(8,128)(2,1)} %constant.19.clone.mat_lo) | copy-start | bytes 393220
  11.0 30.0 %copy-start.7 = (f32[34,128]{1,0:T(8,128)S(1)}, f32[34,128]{1,0:T(8,128)}, u32[]{:S(2)}) copy-start(f32[34,128]{1,0:T(8,128)} %constant.20.clone.tw_ref.tw_scaled) | copy-start | bytes 52228
  35.6 29.8 %all-to-all-start.1 = ((bf16[16,2,128,128]{3,2,1,0:T(8,128)(2,1)}), bf16[16,2,128,128]{3,2,1,0:T(8,128)(2,1)S(1)}, u32[]{:S(2)}, u32[]{:S(2)}) async-start(bf16[16,2,128,128]{3,2,1,0:T(8,128)(2,1)} %pad_maximum_fusion), calls=%async_computation.1 | async-start | bytes 2097152 | tf_op jit(solution)/shard_map/all_to_all | solution.py:306
  41.0 1.2 %copy-start.2 = (f32[128,2048]{1,0:T(8,128)S(1)}, f32[128,2048]{1,0:T(8,128)}, u32[]{:S(2)}) copy-start(f32[128,2048]{1,0:T(8,128)} %two_ref.1) | copy-start | bytes 3145732
  42.2 0.9 copy-start.4
  43.1 5.8 %copy-start.5 = (bf16[256,256]{1,0:T(8,128)(2,1)S(1)}, bf16[256,256]{1,0:T(8,128)(2,1)}, u32[]{:S(2)}) copy-start(bf16[256,256]{1,0:T(8,128)(2,1)} %constant.18.clone.mat_hi) | copy-start | bytes 393220
  43.1 5.8 %copy-start.8 = (f32[34,128]{1,0:T(8,128)S(1)}, f32[34,128]{1,0:T(8,128)}, u32[]{:S(2)}) copy-start(f32[34,128]{1,0:T(8,128)} %constant.21.clone.tw_ref) | copy-start | bytes 52228
  47.5 1.4 %copy-start.9 = (f32[2176,256]{1,0:T(8,128)}, f32[2176,256]{1,0:T(8,128)S(1)}, u32[]{:S(2)}) copy-start(f32[2176,256]{1,0:T(8,128)S(1)} %get-tuple-element.18.h_one) | copy-start | bytes 6684676
  48.9 21.5 %copy-start.6 = (bf16[256,256]{1,0:T(8,128)(2,1)S(1)}, bf16[256,256]{1,0:T(8,128)(2,1)}, u32[]{:S(2)}) copy-start(bf16[256,256]{1,0:T(8,128)(2,1)} %constant.18.clone.mat_hi) | copy-start | bytes 393220
  61.3 1.4 %copy-start.10 = (f32[2176,256]{1,0:T(8,128)}, f32[2176,256]{1,0:T(8,128)S(1)}, u32[]{:S(2)}) copy-start(f32[2176,256]{1,0:T(8,128)S(1)} %get-tuple-element.23.spec_two) | copy-start | bytes 6684676
  62.7 1.4 %copy-start.12 = (f32[2176,256]{1,0:T(8,128)}, f32[2176,256]{1,0:T(8,128)S(1)}, u32[]{:S(2)}) copy-start(f32[2176,256]{1,0:T(8,128)S(1)} %get-tuple-element.24.spec_one) | copy-start | bytes 6684676
  65.4 29.8 %all-to-all-start.2 = ((bf16[16,2,128,128]{3,2,1,0:T(8,128)(2,1)}), bf16[16,2,128,128]{3,2,1,0:T(8,128)(2,1)S(1)}, u32[]{:S(2)}, u32[]{:S(2)}) async-start(bf16[16,2,128,128]{3,2,1,0:T(8,128)(2,1)} %get-tuple-element.21), calls=%async_computation.2 | async-start | bytes 2097152 | tf_op jit(solution)/shard_map/all_to_all | solution.py:306
  70.4 1.6 %copy-start.11 = (f32[2176,256]{1,0:T(8,128)S(1)}, f32[2176,256]{1,0:T(8,128)}, u32[]{:S(2)}) copy-start(f32[2176,256]{1,0:T(8,128)} %copy-done.10) | copy-start | bytes 6684676
  72.0 1.6 %copy-start.13 = (f32[2176,256]{1,0:T(8,128)S(1)}, f32[2176,256]{1,0:T(8,128)}, u32[]{:S(2)}) copy-start(f32[2176,256]{1,0:T(8,128)} %copy-done.12) | copy-start | bytes 6684676
  83.3 12.8 %copy-start.15 = (bf16[2048,128]{1,0:T(8,128)(2,1)S(1)}, bf16[2048,128]{1,0:T(8,128)(2,1)}, u32[]{:S(2)}) copy-start(bf16[2048,128]{1,0:T(8,128)(2,1)} %param.18) | copy-start | bytes 1572868
where the time goes:
time: 97.7 us; the launch traced here: 97.1 us
  waiting for transfers between devices  35.8 us (37%)
  Pallas kernels  26.4 us (27%)
  starting transfers between devices  16.6 us (17%)
  local copies, waits for them, and re-layouts  10.8 us (11%)
  other arithmetic  6.82 us (7%)
    all_to_all x3, waiting for transfers between devices, exchange(): return lax.all_to_all(value, 'seq', split_axis=0, concat_axis=0, tiled=True)  35.8 us
    pallas_call x3, Pallas kernels, call(): pl.pallas_call(kernel, out_shape=out_shape, in_specs=[vmem] * len(args),...  26.4 us
    all_to_all x3, starting transfers between devices, exchange(): return lax.all_to_all(value, 'seq', split_axis=0, concat_axis=0, tiled=True)  16.6 us
    unnamed x39, local copies, waits for them, and re-layouts  9.7 us
    convert_element_type x3, other arithmetic, product(): return (a.astype(F32) * b.astype(F32)).astype(BF16)  3.55 us
    another operation x1, other arithmetic, local(): second_in = jnp.stack([inner, value.reshape(shape)], axis=1)  2.21 us
  transfers between devices with their start and end apart: 3, of which 3 were waited for; matrix products, arithmetic and copies ran while one was open for 3% of the time, Pallas kernels for 27%

commit v1 on v0

v1 whole, which is shorter than its diff:
```python
import functools
import math

import jax
import jax.numpy as jnp
import numpy as np
from jax import lax
from jax.experimental import pallas as pl
from jax.experimental.pallas import tpu as pltpu
from jax.sharding import PartitionSpec as P

F32 = jnp.float32
BF16 = jnp.bfloat16
ROWS = 16
SPARE = 6 * 1024 * 1024
WHOLE = 64128 * 1024
PARTS = 4
TILE = 272


def cmul_const(x, angle, gain=1.0):
    re, im = x
    c, s = gain * math.cos(angle), gain * math.sin(angle)
    if abs(s) < 1e-12:
        if abs(c - 1.0) < 1e-12:
            return x
        return (re * c, im * c)
    if abs(c) < 1e-12:
        if abs(s + 1.0) < 1e-12:
            return (im, -re)
        if abs(s - 1.0) < 1e-12:
            return (-im, re)
    if abs(abs(c) - abs(s)) < 1e-12:
        m = abs(c)
        sc, ss = (1.0 if c > 0 else -1.0), (1.0 if s > 0 else -1.0)
        a = (re - im) if sc * ss > 0 else (re + im)
        b = (re + im) if sc * ss > 0 else (im - re)
        return (a * (m * sc), b * (m * sc))
    return (re * c - im * s, re * s + im * c)


def cdft(xs, sign):
    n = len(xs)
    if n == 1:
        return list(xs)
    even, odd = cdft(xs[0::2], sign), cdft(xs[1::2], sign)
    half = n // 2
    low, high = [], []
    for k in range(half):
        (er, ei), (tr, ti) = even[k], cmul_const(odd[k], sign * 2.0 * math.pi * k / n)
        low.append((er + tr, ei + ti))
        high.append((er - tr, ei - ti))
    return low + high


def odd_part(y, n):
    quarter = n // 4
    u = [cmul_const((y[j], -y[j + quarter]), -2.0 * math.pi * j / n) for j in range(quarter)]
    out = {}
    for p, (re, im) in enumerate(cdft(u, -1)):
        k = 4 * p + 1
        if k <= n // 2:
            out[k] = (re, im)
        else:
            out[n - k] = (re, -im)
    return out


def rdft(xs):
    n = len(xs)
    if n == 1:
        return [(xs[0], None)]
    half = n // 2
    even = rdft([xs[j] + xs[j + half] for j in range(half)])
    if n == 2:
        return [even[0], (xs[0] - xs[1], None)]
    odd = odd_part([xs[j] - xs[j + half] for j in range(half)], n)
    return [even[k // 2] if k % 2 == 0 else odd[k] for k in range(half + 1)]


def rdft_padded(xs):
    n = 2 * len(xs)
    even, odd = rdft(xs), odd_part(xs, n)
    return [even[k // 2] if k % 2 == 0 else odd[k] for k in range(len(xs) + 1)]


def odd_back(spec, n):
    quarter = n // 4
    u = []
    for p in range(quarter):
        k = 4 * p + 1
        if k <= n // 2:
            u.append(spec[k])
        else:
            re, im = spec[n - k]
            u.append((re, -im))
    v = cdft(u, 1)
    low, high = [], []
    for j in range(quarter):
        re, im = cmul_const(v[j], 2.0 * math.pi * j / n, 2.0)
        low.append(re)
        high.append(-im)
    return low + high


def irdft(spec):
    n = 2 * (len(spec) - 1)
    if n == 2:
        a, b = spec[0][0], spec[1][0]
        return [a + b, a - b]
    even, odd = irdft(spec[0::2]), odd_back(spec, n)
    return [e + o for e, o in zip(even, odd)] + [e - o for e, o in zip(even, odd)]


def irdft_half(spec):
    n = 2 * (len(spec) - 1)
    even, odd = irdft(spec[0::2]), odd_back(spec, n)
    return [e + o for e, o in zip(even, odd)]


def split(x):
    hi = x.astype(BF16)
    return hi, (x - hi.astype(F32)).astype(BF16)


def tables(blocks, width, scale):
    k1 = np.arange(blocks + 1, dtype=np.float64)[:, None]
    f = np.arange(width, dtype=np.float64)
    total = 2 * blocks * width
    angle = 2.0 * np.pi * (k1 * f[None, :]) / total
    twiddle = np.stack([np.cos(angle), -np.sin(angle)], axis=1).reshape(-1, width)
    theta = 2.0 * np.pi * ((f[:, None] * f[None, :]) % width) / width
    c, s = np.cos(theta), np.sin(theta)
    matrix = np.block([[c, -s], [s, c]]).astype(np.float32)
    hi = matrix.astype(jnp.bfloat16)
    lo = (matrix - hi.astype(np.float32)).astype(jnp.bfloat16)
    return hi, lo, twiddle.astype(np.float32), (twiddle * scale).astype(np.float32)


def spread(xs, twiddle_ref, hi_ref, lo_ref):
    width = xs[0].shape[1]
    for k, (re, im) in enumerate(rdft_padded(xs)):
        c = twiddle_ref[2 * k : 2 * k + 1, :]
        s = twiddle_ref[2 * k + 1 : 2 * k + 2, :]
        if im is None:
            tr, ti = re * c, re * s
        else:
            tr, ti = re * c - im * s, re * s + im * c
        for value, at in ((tr, 0), (ti, width)):
            hi, lo = split(value)
            hi_ref[k * ROWS : (k + 1) * ROWS, at : at + width] = hi
            lo_ref[k * ROWS : (k + 1) * ROWS, at : at + width] = lo


def gather(spec_ref, twiddle_ref, width):
    spec = []
    last = spec_ref.shape[0] // ROWS - 1
    for k in range(last + 1):
        rows = slice(k * ROWS, (k + 1) * ROWS)
        re, im = spec_ref[rows, :width], spec_ref[rows, width:]
        c = twiddle_ref[2 * k : 2 * k + 1, :]
        s = twiddle_ref[2 * k + 1 : 2 * k + 2, :]
        if k == 0 or k == last:
            spec.append((re * c + im * s, None))
        else:
            spec.append((re * c + im * s, im * c - re * s))
    return irdft_half(spec)


def dot3(hi, lo, mat_hi, mat_lo, dims):
    def dot(a, b):
        return lax.dot_general(a, b, (dims, ((), ())), preferred_element_type=F32)

    return dot(hi, mat_hi) + dot(lo, mat_hi) + dot(hi, mat_lo)


FORWARD = ((1,), (0,))
BACK = ((1,), (1,))


def tiles(rows):
    size = TILE if rows % TILE == 0 else rows
    return [slice(at, at + size) for at in range(0, rows, size)]


def multiply_back(spec, other, mat_hi, mat_lo, width):
    gr, gi = spec[:, :width], spec[:, width:]
    hr, hi = other[:, :width], other[:, width:]
    zr, zi = gr * hr + gi * hi, gi * hr - gr * hi
    z_hi, z_lo = split(jnp.concatenate([zr, zi], axis=1))
    return dot3(z_hi, z_lo, mat_hi[...], mat_lo[...], BACK)


def staggered(groups, stages):
    for t in range(groups + len(stages) - 1):
        for s in reversed(range(len(stages))):
            if 0 <= t - s < groups:
                stages[s](t - s)


def spectrum_kernel(blocks, width, one_ref, two_ref, mat_hi, mat_lo, tw_ref, out_one, out_two,
                    hi_ref, lo_ref):
    groups = one_ref.shape[0] // ROWS

    def source(g):
        refs = (two_ref, out_two) if g < groups else (one_ref, out_one)
        return refs + (g % groups,)

    def load(g):
        filt, _, at = source(g)
        rows = slice(at * ROWS, (at + 1) * ROWS)
        xs = [filt[rows, b * width : (b + 1) * width] for b in range(blocks)]
        spread(xs, tw_ref, hi_ref.at[g % 2], lo_ref.at[g % 2])

    def transform(g):
        _, out, at = source(g)
        for here in tiles(hi_ref.shape[1]):
            out[at, here, :] = dot3(hi_ref[g % 2, here, :], lo_ref[g % 2, here, :], mat_hi[...],
                                    mat_lo[...], FORWARD)

    staggered(2 * groups, [load, transform])


def adjoint_kernel(blocks, width, sent, filt_two, filt_one, skip_two, skip_one, taps_ref,
                   mat_hi, mat_lo, tw_ref, back_far, grad_far,
                   hi_two, lo_two, back_two, hi_one, lo_one, back_one,
                   in_ref, h_two, h_one, out_ref, grad_ref, sems):
    groups = h_two.shape[0]
    parts = math.gcd(groups, PARTS)
    each = groups // parts

    def moves(part):
        some = pl.ds(part * each, each)
        rows = pl.ds(part * each * ROWS, each * ROWS)
        pairs = (
            (sent.at[:, pl.ds(0, 2), rows, :], in_ref.at[:, :, rows, :]),
            (filt_two.at[some], h_two.at[some]),
            (filt_one.at[some], h_one.at[some]),
            (grad_ref.at[:, rows, :], grad_far.at[:, rows, :]),
            (out_ref.at[:, 0, rows, :], back_far.at[:, 0, rows, :]),
            (out_ref.at[:, 1, rows, :], back_far.at[:, 1, rows, :]),
        )
        return [pltpu.make_async_copy(source, target, sems.at[part * len(pairs) + i])
                for i, (source, target) in enumerate(pairs)]

    copies = [moves(part) for part in range(parts)]
    for index in (0, 1, 2):
        for copy in copies:
            copy[index].start()

    def begin(g, index):
        if g == 0:
            for copy in copies:
                copy[index].wait()

    def end(g, index):
        if g == groups - 1:
            for copy in copies:
                copy[index].start()

    lane = lax.broadcasted_iota(jnp.int32, (ROWS, width), 1)
    count = taps_ref.shape[1]

    def rows_of(g):
        return slice(g * ROWS, (g + 1) * ROWS)

    def convolve(g, h_ref, hi_ref, lo_ref, back_ref):
        p = g % 2
        for here in tiles(hi_ref.shape[1]):
            spec = dot3(hi_ref[p, here, :], lo_ref[p, here, :], mat_hi[...], mat_lo[...], FORWARD)
            back_ref[p, here, :] = multiply_back(spec, h_ref[g, here, :], mat_hi, mat_lo, width)

    def load(g):
        begin(g, 0)
        here = rows_of(g)
        xs = [in_ref[b, 0, here, :].astype(F32) for b in range(blocks)]
        spread(xs, tw_ref, hi_two.at[g % 2], lo_two.at[g % 2])

    def first(g):
        begin(g, 1)
        convolve(g, h_two, hi_two, lo_two, back_two)

    def between(g):
        here = rows_of(g)
        skip = skip_two[here, :]
        back = gather(back_two.at[g % 2], tw_ref, width)
        grads = []
        for b in range(blocks):
            full = back[b] + skip * in_ref[b, 0, here, :].astype(F32)
            grad = full.astype(BF16)
            out_ref[b, 0, here, :] = grad
            grad = (grad.astype(F32) * in_ref[b, 1, here, :].astype(F32)).astype(BF16)
            grad_ref[b, here, :] = grad
            grads.append(grad.astype(F32))
        end(g, 3)
        end(g, 4)
        spread(grads, tw_ref, hi_one.at[g % 2], lo_one.at[g % 2])

    def second(g):
        begin(g, 2)
        convolve(g, h_one, hi_one, lo_one, back_one)

    def finish(g):
        here = rows_of(g)
        skip = skip_one[here, :]
        back = gather(back_one.at[g % 2], tw_ref, width)
        grads = []
        for b in range(blocks):
            full = back[b] + skip * grad_ref[b, here, :].astype(F32)
            grads.append(full.astype(BF16).astype(F32))
        grads.append(jnp.zeros((ROWS, width), F32))
        sums = [taps_ref[here, 0:1] * grads[b] for b in range(blocks)]
        for k in range(1, count):
            turned = [pltpu.roll(v, width - k, 1) for v in grads]
            for b in range(blocks):
                moved = jnp.where(lane < width - k, turned[b], turned[b + 1])
                sums[b] = sums[b] + taps_ref[here, k : k + 1] * moved
        for b in range(blocks):
            out_ref[b, 1, here, :] = sums[b].astype(BF16)
        end(g, 5)

    staggered(groups, [load, first, between, second, finish])
    for copy in copies:
        for index in (3, 4, 5):
            copy[index].wait()


def filter_kernel(blocks, width, me_ref, in_ref, inner_ref, grad_ref, mat_hi, mat_lo, tw_ref, tw_scaled,
                  out_one, out_two, hi_ref, lo_ref, other_hi, other_lo, back_ref):
    groups = grad_ref.shape[1] // ROWS
    me = me_ref[0]

    def load(g):
        p = g % 2
        rows = slice((g % groups) * ROWS, (g % groups + 1) * ROWS)
        if g < groups:
            xs = [in_ref[b, 2, rows, :].astype(F32) for b in range(blocks)]
            grads = [grad_ref[b, rows, :].astype(F32) for b in range(blocks)]
        else:
            xs = [inner_ref[me ^ b, rows, :].astype(F32) for b in range(blocks)]
            grads = [in_ref[b, 0, rows, :].astype(F32) for b in range(blocks)]
        spread(xs, tw_scaled, other_hi.at[p], other_lo.at[p])
        spread(grads, tw_ref, hi_ref.at[p], lo_ref.at[p])

    def transform(g):
        p = g % 2
        for here in tiles(hi_ref.shape[1]):
            spec = dot3(hi_ref[p, here, :], lo_ref[p, here, :], mat_hi[...], mat_lo[...], FORWARD)
            other = dot3(other_hi[p, here, :], other_lo[p, here, :], mat_hi[...], mat_lo[...],
                         FORWARD)
            back_ref[p, here, :] = multiply_back(spec, other, mat_hi, mat_lo, width)

    def finish(g):
        out = out_one if g < groups else out_two
        rows = slice((g % groups) * ROWS, (g % groups + 1) * ROWS)
        back = gather(back_ref.at[g % 2], tw_ref, width)
        for b in range(blocks):
            out[rows, b * width : (b + 1) * width] = back[b]

    staggered(2 * groups, [load, transform, finish])


def product(a, b):
    return (a.astype(F32) * b.astype(F32)).astype(BF16)


def send_kernel(out_grad, gate_two, gate_one, value, out, *refs):
    held, made, sems = refs[:4], refs[4], refs[5]
    blocks = out_grad.shape[0]
    parts = math.gcd(blocks, PARTS)
    step = blocks // parts
    arrive, leave = [], []
    for part in range(parts):
        here = pl.ds(part * step, step)
        arrive.append([pltpu.make_async_copy(ref.at[here], to.at[here], sems.at[7 * part + i])
                       for i, (ref, to) in enumerate(zip((out_grad, gate_two, gate_one, value), held))])
        leave.append([pltpu.make_async_copy(ref.at[here], out.at[here, i],
                                            sems.at[7 * part + 4 + i])
                      for i, ref in enumerate((made, held[2], held[3]))])
    for copies in arrive:
        for copy in copies:
            copy.start()
    for part in range(parts):
        here = slice(part * step, (part + 1) * step)
        for i in (2, 3):
            arrive[part][i].wait()
            leave[part][i - 1].start()
        for i in (0, 1):
            arrive[part][i].wait()
        made[here] = product(held[0][here], held[1][here])
        leave[part][0].start()
    for copies in leave:
        for copy in copies:
            copy.wait()


def receive_kernel(came, conv_one, proj_grad, gate_one_grad, made, sems):
    blocks = conv_one.shape[0]
    parts = math.gcd(blocks, PARTS)
    step = blocks // parts
    copies = [pltpu.make_async_copy(came.at[:, 1], proj_grad, sems.at[parts])]
    copies[0].start()
    for part in range(parts):
        here = pl.ds(part * step, step)
        made[here] = product(came[here, 0], conv_one[here])
        copies.append(pltpu.make_async_copy(made.at[here], gate_one_grad.at[here], sems.at[part]))
        copies[-1].start()
    for copy in copies:
        copy.wait()


def call(kernel, out_shape, scratch, flops, moved, *args, far=(), far_out=False, copies=0,
         limit=0):
    vmem = pl.BlockSpec(memory_space=pltpu.VMEM)
    smem = pl.BlockSpec(memory_space=pltpu.SMEM)
    hbm = pl.BlockSpec(memory_space=pltpu.HBM)
    held = sum(math.prod(dims) * np.dtype(dtype).itemsize for dims, dtype in scratch)
    buffers = [pltpu.VMEM(dims, dtype) for dims, dtype in scratch]
    if copies:
        buffers.append(pltpu.SemaphoreType.DMA((copies,)))
    return pl.pallas_call(
        kernel,
        out_shape=out_shape,
        in_specs=[smem if a.dtype == jnp.int32 else hbm if i in far else vmem
                  for i, a in enumerate(args)],
        out_specs=[hbm if far_out else vmem] * len(out_shape),
        scratch_shapes=buffers,
        compiler_params=pltpu.CompilerParams(
            vmem_limit_bytes=limit or held + SPARE),
        cost_estimate=pl.CostEstimate(flops=flops, bytes_accessed=moved, transcendentals=0),
    )(*args)


def exchange(value):
    return lax.all_to_all(value, "seq", split_axis=0, concat_axis=0, tiled=True)


def swap(value, step):
    count = lax.axis_size("seq")
    return lax.ppermute(value, "seq", [(j, j ^ step) for j in range(count)])


def exchange_near(value):
    me = lax.axis_index("seq")
    half = value.shape[0] // 2
    value = value.reshape((2, half) + value.shape[1:])
    mine = me // half
    value = jnp.concatenate(
        [lax.dynamic_index_in_dim(value, mine, 0), lax.dynamic_index_in_dim(value, 1 - mine, 0)])
    parts = [lax.dynamic_index_in_dim(value, (me % half) ^ r, 1) for r in range(half)]
    parts = lax.optimization_barrier(tuple(parts))
    came = [parts[0]] + [swap(parts[r], r) for r in range(1, half)]
    return ([part[0] for part in came], jnp.concatenate([part[1] for part in came]))


def local(
    out_grad,
    gate_one,
    gate_two,
    conv_one,
    conv_two,
    value,
    filter_one,
    filter_two,
    skip_one,
    skip_two,
    short_weight,
):
    blocks = lax.axis_size("seq")
    width = out_grad.shape[1]
    channels = filter_one.shape[0]
    length = filter_one.shape[1]
    rows = (blocks + 1) * channels
    shape = (blocks, channels, width)
    mat_hi, mat_lo, tw, tw_scaled = tables(
        blocks, width, length ** (-0.5) / (2 * length))
    work = 3 * 2 * rows * (2 * width) ** 2
    size = rows * 2 * width * 4

    def struct(*dims, dtype=F32):
        return jax.ShapeDtypeStruct(dims, dtype)

    groups = channels // ROWS
    tile = ((blocks + 1) * ROWS, 2 * width)
    halves = [((2,) + tile, BF16)] * 2
    back = ((2,) + tile, F32)
    spec = struct(groups, *tile)

    me = lax.axis_index("seq")
    taps = lax.dynamic_slice_in_dim(short_weight, me * channels, channels, axis=0)
    pair = struct(blocks, 2, channels, width, dtype=BF16)
    parts = math.gcd(blocks, PARTS)
    one = struct(*shape, dtype=BF16)
    triple = struct(blocks, 3, channels, width, dtype=BF16)
    first = exchange(call(
        send_kernel, [triple], [(shape, BF16)] * 5, 3 * pair.size, 7 * pair.size,
        *(a.reshape(shape) for a in (out_grad, gate_two, gate_one, value)),
        far=range(4), far_out=True, copies=7 * parts, limit=WHOLE)[0])
    near, far = exchange_near(product(gate_one, conv_one).reshape(shape))
    h_one, h_two = call(
        functools.partial(spectrum_kernel, blocks, width),
        [spec, spec], halves, 2 * work, 4 * size,
        filter_one, filter_two, mat_hi, mat_lo, tw_scaled)
    gate_two_grad = product(out_grad, conv_two)
    far = swap(far, blocks // 2)
    first, h_one, h_two, gate_two_grad = lax.optimization_barrier(
        (first, h_one, h_two, gate_two_grad))
    grads, cg_one = call(
        functools.partial(adjoint_kernel, blocks, width),
        [pair, struct(*shape, dtype=BF16)],
        (halves + [back]) * 2 + [(pair.shape, BF16)] + [((groups,) + tile, F32)] * 2
        + [(pair.shape, BF16), (shape, BF16)],
        4 * work, 8 * size,
        first, h_two, h_one, skip_two[:, None], skip_one[:, None], taps, mat_hi, mat_lo, tw,
        far=(0, 1, 2), far_out=True, copies=6 * math.gcd(groups, PARTS), limit=WHOLE)
    grads, far = lax.optimization_barrier((grads, far))
    inner = jnp.concatenate(near + [far])
    third = exchange(grads)
    filter_one_grad, filter_two_grad = call(
        functools.partial(filter_kernel, blocks, width),
        [struct(channels, length), struct(channels, length)],
        halves * 2 + [back], 6 * work, 8 * size,
        me[None].astype(jnp.int32), first, inner, cg_one, mat_hi, mat_lo, tw, tw_scaled)
    proj_grad, gate_one_grad = call(
        receive_kernel, [one, one], [(shape, BF16)], pair.size, 6 * pair.size,
        third, conv_one.reshape(shape), far_out=True, copies=parts + 1)
    proj_grad = proj_grad.reshape(out_grad.shape)
    gate_one_grad = gate_one_grad.reshape(out_grad.shape)
    return (proj_grad, gate_one_grad, gate_two_grad, filter_one_grad, filter_two_grad)


def solution(mesh):
    frames = P(None, ("groups", "seq"))
    return jax.shard_map(
        local,
        mesh=mesh,
        in_specs=(frames,) * 6 + (P("seq", None),) * 2 + (P("seq"),) * 2 + (P(),),
        out_specs=(frames,) * 3 + (P(("groups", "seq"), None),) * 2,
        check_vma=False,
    )
```

time: 97.7 us -> 91.3 us (0.934)
  waiting for transfers between devices: 35.8 us -> 18.8 us
  local copies, waits for them, and re-layouts: 10.8 us -> 16 us
  starting transfers between devices: 16.6 us -> 21.2 us
  Pallas kernels: 26.4 us -> 30.2 us
  other arithmetic: 6.82 us -> 3.28 us
    all_to_all x3 -> x2, waiting for transfers between devices: 35.8 us -> 12.5 us  [exchange(): return lax.all_to_all(value, 'seq', split_axis=0, concat_axis=0, tiled=True)]
    ppermute x0 -> x8, starting transfers between devices: none -> 6.58 us  [swap(): return lax.ppermute(value, 'seq', [(j, j ^ step) for j in range(count)])]
    ppermute x0 -> x8, waiting for transfers between devices: none -> 6.33 us  [swap(): return lax.ppermute(value, 'seq', [(j, j ^ step) for j in range(count)])]
    pallas_call x3 -> x5, Pallas kernels: 26.4 us -> 30.2 us  [call(): pl.pallas_call(kernel, out_shape=out_shape, in_specs=[smem if a.dtype ==...]
    another operation x2 -> x0, other arithmetic: 3.27 us -> none  [the longest x1 2.21 us: local(): second_in = jnp.stack([inner, value.reshape(shape)], axis=1)]
    unnamed x39 -> x45, local copies, waits for them, and re-layouts: 9.7 us -> 12.5 us
    all_to_all x3 -> x2, starting transfers between devices: 16.6 us -> 14.6 us  [exchange(): return lax.all_to_all(value, 'seq', split_axis=0, concat_axis=0, tiled=True)]
    convert_element_type x3 -> x2, other arithmetic: 3.55 us -> 1.86 us  [product(): return (a.astype(F32) * b.astype(F32)).astype(BF16)]
  transfers between devices with their start and end apart: 3 -> 10, of which waited for: 3 -> 6; matrix products, arithmetic and copies ran while one was open for 3% -> 18% of each run, Pallas kernels for 27% -> 29%
where the time goes in v1:
time: 91.3 us; the launch traced here: 90.6 us
  Pallas kernels  30.2 us (33%)
  starting transfers between devices  21.2 us (23%)
  waiting for transfers between devices  18.8 us (21%)
  local copies, waits for them, and re-layouts  16 us (18%)
  other arithmetic  3.28 us (4%)
  between operations  1.05 us (1%)
    pallas_call x5, Pallas kernels, call(): pl.pallas_call(kernel, out_shape=out_shape, in_specs=[smem if a.dtype ==...  30.2 us
    all_to_all x2, starting transfers between devices, exchange(): return lax.all_to_all(value, 'seq', split_axis=0, concat_axis=0, tiled=True)  14.6 us
    unnamed x45, local copies, waits for them, and re-layouts  12.5 us
    all_to_all x2, waiting for transfers between devices, exchange(): return lax.all_to_all(value, 'seq', split_axis=0, concat_axis=0, tiled=True)  12.5 us
    ppermute x8, starting transfers between devices, swap(): return lax.ppermute(value, 'seq', [(j, j ^ step) for j in range(count)])  6.58 us
    ppermute x8, waiting for transfers between devices, swap(): return lax.ppermute(value, 'seq', [(j, j ^ step) for j in range(count)])  6.33 us
    convert_element_type x2, other arithmetic, product(): return (a.astype(F32) * b.astype(F32)).astype(BF16)  1.86 us
  transfers between devices with their start and end apart: 10, of which 6 were waited for; matrix products, arithmetic and copies ran while one was open for 18% of the time, Pallas kernels for 29%

profile of v1, /device:TPU:9, one launch (start us, length us, event | category | flops | bytes accessed | tf_op | source)
XLA Modules:
  0.0 90.6 jit_solution(17873250132749544586)
XLA Ops:
  0.6 2.6 %shard_map.182 = bf16[16,3,128,128]{3,2,1,0:T(8,128)(2,1)} custom-call(bf16[16,128,128]{2,1,0:T(8,128)(2,1)} %bitcast.73, bf16[16,128,128]{2,1,0:T(8,128)(2,1)} %bitcast.75, bf16[16,128,128]{2,1,0:T(8,128)(2,1)} %bitcast.72, bf16[16,128,128]{2,1,0:T(8,128)(2,1)} %bitcast.76), custom_call_target="tpu_custom_call" | custom-call | flops 1572864 | bytes 3670016 | tf_op jit(solution)/shard_map/pallas_call | solution.py:421
  3.3 6.8 %all-to-all-start = ((bf16[16,3,128,128]{3,2,1,0:T(8,128)(2,1)}), bf16[16,3,128,128]{3,2,1,0:T(8,128)(2,1)}, u32[]{:S(2)}, u32[]{:S(2)}) async-start(bf16[16,3,128,128]{3,2,1,0:T(8,128)(2,1)} %shard_map.182), calls=%async_computation | async-start | bytes 3145728 | tf_op jit(solution)/shard_map/all_to_all | solution.py:435
  11.0 1.1 %constant_dynamic-slice_fusion = (bf16[1,8,128,128]{3,2,1,0:T(8,128)(2,1)S(1)}, bf16[1,8,128,128]{3,2,1,0:T(8,128)(2,1)S(1)}) fusion(bf16[2,8,128,128]{3,2,1,0:T(8,128)(2,1)} %bitcast.74, s32[]{:T(128)S(6)} %select_n.63, s32[]{:T(128)S(6)} %select_n.62), kind=kLoop, calls=%fused_computation.57 | loop fusion | bytes 1048584 | tf_op jit(solution)/shard_map/jit(dynamic_index_in_dim)/dynamic_slice | solution.py:449
  13.9 1.2 %collective-permute-start.1 = (bf16[2,1,128,128]{3,2,1,0:T(8,128)(2,1)}, bf16[2,1,128,128]{3,2,1,0:T(8,128)(2,1)}, u32[]{:S(2)}, u32[]{:S(2)}) collective-permute-start(bf16[2,1,128,128]{3,2,1,0:T(8,128)(2,1)} %get-tuple-element.35), channel_id=1, source_target_pairs={{0,2},{1,3},{2,0},{3,1},{4,6},{5,7},{6,4},{7,5},{8,10},{9,11},{10,... | collective-permute-start | bytes 196616 | tf_op jit(solution)/shard_map/ppermute | solution.py:440
  15.8 1.6 %collective-permute-start.4 = (bf16[2,1,128,128]{3,2,1,0:T(8,128)(2,1)}, bf16[2,1,128,128]{3,2,1,0:T(8,128)(2,1)}, u32[]{:S(2)}, u32[]{:S(2)}) collective-permute-start(bf16[2,1,128,128]{3,2,1,0:T(8,128)(2,1)} %get-tuple-element.38), channel_id=1, source_target_pairs={{0,5},{1,4},{2,7},{3,6},{4,1},{5,0},{6,3},{7,2},{8,13},{9,12},{10,... | collective-permute-start | bytes 196616 | tf_op jit(solution)/shard_map/ppermute | solution.py:440
  18.9 3.3 %shard_map.183 = (f32[8,272,256]{2,1,0:T(8,128)S(1)}, f32[8,272,256]{2,1,0:T(8,128)S(1)}) custom-call(f32[128,2048]{1,0:T(8,128)S(1)} %copy-done.2, f32[128,2048]{1,0:T(8,128)S(1)} %copy-done.3, bf16[256,256]{1,0:T(8,128)(2,1)S(1)} %copy-done.4, bf16[256,256]{1,0:T(8,128)(2,1)S(1)} %copy-done.6, f32[34,128]{1,0:T(8,128)S(1)} %copy-done.8), custom_call_target="tpu_custom_call" | custom-call | flops 1711276032 | bytes 8912896 | tf_op jit(solution)/shard_map/pallas_call | solution.py:421
  22.2 1.4 %copy-done.10 = f32[8,272,256]{2,1,0:T(8,128)} copy-done((f32[8,272,256]{2,1,0:T(8,128)}, f32[8,272,256]{2,1,0:T(8,128)S(1)}, u32[]{:S(2)}) %copy-start.10) | copy-done | bytes 2228248
  23.6 1.4 %copy-done.11 = f32[8,272,256]{2,1,0:T(8,128)} copy-done((f32[8,272,256]{2,1,0:T(8,128)}, f32[8,272,256]{2,1,0:T(8,128)S(1)}, u32[]{:S(2)}) %copy-start.11) | copy-done | bytes 2228248
  27.3 1.2 %collective-permute-start.5 = (bf16[2,1,128,128]{3,2,1,0:T(8,128)(2,1)}, bf16[2,1,128,128]{3,2,1,0:T(8,128)(2,1)S(1)}, u32[]{:S(2)}, u32[]{:S(2)}) collective-permute-start(bf16[2,1,128,128]{3,2,1,0:T(8,128)(2,1)} %get-tuple-element.39), channel_id=1, source_target_pairs={{0,6},{1,7},{2,4},{3,5},{4,2},{5,3},{6,0},{7,1},{8,14},{9,15},{10,... | collective-permute-start | bytes 196616 | tf_op jit(solution)/shard_map/ppermute | solution.py:440
  28.5 1.4 %constant_dynamic-update-slice_fusion.15 = (bf16[16,128,128]{2,1,0:T(8,128)(2,1)S(1)}, bf16[8,128,128]{2,1,0:T(8,128)(2,1)}) fusion(bf16[16,128,128]{2,1,0:T(8,128)(2,1)S(1)} %get-tuple-element.73, bf16[2,1,128,128]{3,2,1,0:T(8,128)(2,1)} %collective-permute-done, bf16[8,128,128]{2,1,0:T(8,128)(2,1)} %get-tuple-element.74), kind=kLoop, calls=%fused_computation.41 | loop fusion | bytes 131072
  29.9 1.5 %collective-permute-start.6 = (bf16[2,1,128,128]{3,2,1,0:T(8,128)(2,1)}, bf16[2,1,128,128]{3,2,1,0:T(8,128)(2,1)S(1)}, u32[]{:S(2)}, u32[]{:S(2)}) collective-permute-start(bf16[2,1,128,128]{3,2,1,0:T(8,128)(2,1)} %get-tuple-element.40), channel_id=1, source_target_pairs={{0,7},{1,6},{2,5},{3,4},{4,3},{5,2},{6,1},{7,0},{8,15},{9,14},{10,... | collective-permute-start | bytes 196616 | tf_op jit(solution)/shard_map/ppermute | solution.py:440
  31.4 1.4 %constant_dynamic-update-slice_fusion.14 = (bf16[16,128,128]{2,1,0:T(8,128)(2,1)S(1)}, bf16[8,128,128]{2,1,0:T(8,128)(2,1)}) fusion(bf16[16,128,128]{2,1,0:T(8,128)(2,1)S(1)} %get-tuple-element.71, bf16[2,1,128,128]{3,2,1,0:T(8,128)(2,1)} %collective-permute-done.1, bf16[8,128,128]{2,1,0:T(8,128)(2,1)} %get-tuple-element.72), kind=kLoop, calls=%fused_computation.40 | loop fusion | bytes 131072
  32.8 1.4 %constant_dynamic-update-slice_fusion.13 = (bf16[16,128,128]{2,1,0:T(8,128)(2,1)S(1)}, bf16[8,128,128]{2,1,0:T(8,128)(2,1)}) fusion(bf16[16,128,128]{2,1,0:T(8,128)(2,1)S(1)} %get-tuple-element.69, bf16[2,1,128,128]{3,2,1,0:T(8,128)(2,1)} %collective-permute-done.2, bf16[8,128,128]{2,1,0:T(8,128)(2,1)} %get-tuple-element.70), kind=kLoop, calls=%fused_computation.39 | loop fusion | bytes 131072
  34.2 4.2 %collective-permute-done.3 = bf16[2,1,128,128]{3,2,1,0:T(8,128)(2,1)} collective-permute-done((bf16[2,1,128,128]{3,2,1,0:T(8,128)(2,1)}, bf16[2,1,128,128]{3,2,1,0:T(8,128)(2,1)}, u32[]{:S(2)}, u32[]{:S(2)}) %collective-permute-start.3) | collective-permute-done | bytes 65568 | tf_op jit(solution)/shard_map/ppermute | solution.py:440
  38.4 1.4 %constant_dynamic-update-slice_fusion.12 = (bf16[16,128,128]{2,1,0:T(8,128)(2,1)S(1)}, bf16[8,128,128]{2,1,0:T(8,128)(2,1)}) fusion(bf16[16,128,128]{2,1,0:T(8,128)(2,1)S(1)} %get-tuple-element.67, bf16[2,1,128,128]{3,2,1,0:T(8,128)(2,1)} %collective-permute-done.3, bf16[8,128,128]{2,1,0:T(8,128)(2,1)} %get-tuple-element.68), kind=kLoop, calls=%fused_computation.38 | loop fusion | bytes 131072
  39.9 1.4 %constant_dynamic-update-slice_fusion.11 = (bf16[16,128,128]{2,1,0:T(8,128)(2,1)S(1)}, bf16[8,128,128]{2,1,0:T(8,128)(2,1)}) fusion(bf16[16,128,128]{2,1,0:T(8,128)(2,1)S(1)} %get-tuple-element.65, bf16[2,1,128,128]{3,2,1,0:T(8,128)(2,1)} %collective-permute-done.4, bf16[8,128,128]{2,1,0:T(8,128)(2,1)} %get-tuple-element.66), kind=kLoop, calls=%fused_computation.37 | loop fusion | bytes 131072
  42.5 1.4 %collective-permute-done.6 = bf16[2,1,128,128]{3,2,1,0:T(8,128)(2,1)S(1)} collective-permute-done((bf16[2,1,128,128]{3,2,1,0:T(8,128)(2,1)}, bf16[2,1,128,128]{3,2,1,0:T(8,128)(2,1)S(1)}, u32[]{:S(2)}, u32[]{:S(2)}) %collective-permute-start.6) | collective-permute-done | bytes 65568 | tf_op jit(solution)/shard_map/ppermute | solution.py:440
  44.6 1.5 %all-to-all-done.sent.in_ref = bf16[16,3,128,128]{3,2,1,0:T(8,128)(2,1)} async-done(((bf16[16,3,128,128]{3,2,1,0:T(8,128)(2,1)}), bf16[16,3,128,128]{3,2,1,0:T(8,128)(2,1)}, u32[]{:S(2)}, u32[]{:S(2)}) %all-to-all-start) | async-done | bytes 1572896 | tf_op jit(solution)/shard_map/all_to_all | solution.py:435
  46.1 10.5 %shard_map.184 = (bf16[16,2,128,128]{3,2,1,0:T(8,128)(2,1)}, bf16[16,128,128]{2,1,0:T(8,128)(2,1)}) custom-call(bf16[16,3,128,128]{3,2,1,0:T(8,128)(2,1)} %all-to-all-done.sent.in_ref, f32[8,272,256]{2,1,0:T(8,128)} %copy-done.11, f32[8,272,256]{2,1,0:T(8,128)} %copy-done.10, f32[128,1]{1,0:T(8,128)} %copy.21.skip_two, f32[128,1]{1,0:T(8,128)} %copy.22.skip_one, ...), custom_call_target="tpu_custom_call" | custom-call | flops 3422552064 | bytes 17825792 | tf_op jit(solution)/shard_map/pallas_call | solution.py:421
  56.7 7.9 %all-to-all-start.1 = ((bf16[16,2,128,128]{3,2,1,0:T(8,128)(2,1)}), bf16[16,2,128,128]{3,2,1,0:T(8,128)(2,1)S(1)}, u32[]{:S(2)}, u32[]{:S(2)}) async-start(bf16[16,2,128,128]{3,2,1,0:T(8,128)(2,1)} %get-tuple-element.41), calls=%async_computation.1 | async-start | bytes 2097152 | tf_op jit(solution)/shard_map/all_to_all | solution.py:435
  64.5 1.0 %constant_dynamic-update-slice_fusion.8.inner_ref = bf16[16,128,128]{2,1,0:T(8,128)(2,1)S(1)} fusion(bf16[16,128,128]{2,1,0:T(8,128)(2,1)S(1)} %get-tuple-element.59, bf16[8,128,128]{2,1,0:T(8,128)(2,1)} %collective-permute-done.7), kind=kLoop, calls=%fused_computation.34 | loop fusion | bytes 524288 | tf_op jit(solution)/shard_map/concatenate | solution.py:517
  65.6 12.9 %shard_map.186 = (f32[128,2048]{1,0:T(8,128)}, f32[128,2048]{1,0:T(8,128)}) custom-call(s32[1]{0:T(128)} %bitcast.18.me_ref, bf16[16,3,128,128]{3,2,1,0:T(8,128)(2,1)} %all-to-all-done.sent.in_ref, bf16[16,128,128]{2,1,0:T(8,128)(2,1)S(1)} %constant_dynamic-update-slice_fusion.8.inner_ref, bf16[16,128,128]{2,1,0:T(8,128)(2,1)S(1)} %copy-done.12, ...), custom_call_target="tpu_custom_call" | custom-call | flops 5133828096 | bytes 17825792 | tf_op jit(solution)/shard_map/pallas_call | solution.py:421
  78.4 11.0 %all-to-all-done.1.came = bf16[16,2,128,128]{3,2,1,0:T(8,128)(2,1)S(1)} async-done(((bf16[16,2,128,128]{3,2,1,0:T(8,128)(2,1)}), bf16[16,2,128,128]{3,2,1,0:T(8,128)(2,1)S(1)}, u32[]{:S(2)}, u32[]{:S(2)}) %all-to-all-start.1) | async-done | bytes 1048608 | tf_op jit(solution)/shard_map/all_to_all | solution.py:435
  89.4 1.0 %shard_map.185 = (bf16[16,128,128]{2,1,0:T(8,128)(2,1)}, bf16[16,128,128]{2,1,0:T(8,128)(2,1)}) custom-call(bf16[16,2,128,128]{3,2,1,0:T(8,128)(2,1)S(1)} %all-to-all-done.1.came, bf16[16,128,128]{2,1,0:T(8,128)(2,1)S(1)} %bitcast.71), custom_call_target="tpu_custom_call" | custom-call | flops 524288 | bytes 3145728 | tf_op jit(solution)/shard_map/pallas_call | solution.py:421
  (55 shorter events, 9.2 us)
Async XLA Ops:
  0.6 25.9 %copy-start = (f32[2048,3]{0,1:T(4,128)S(1)}, f32[2048,3]{0,1:T(4,128)}, u32[]{:S(2)}) copy-start(f32[2048,3]{0,1:T(4,128)} %param.25) | copy-start | bytes 73732
  3.2 6.8 %copy-start.1 = (bf16[2048,128]{1,0:T(8,128)(2,1)S(1)}, bf16[2048,128]{1,0:T(8,128)(2,1)}, u32[]{:S(2)}) copy-start(bf16[2048,128]{1,0:T(8,128)(2,1)} %param.18) | copy-start | bytes 1572868
  3.2 6.8 %copy-start.13 = (bf16[2048,128]{1,0:T(8,128)(2,1)S(1)}, bf16[2048,128]{1,0:T(8,128)(2,1)}, u32[]{:S(2)}) copy-start(bf16[2048,128]{1,0:T(8,128)(2,1)} %param.16) | copy-start | bytes 1572868
  3.3 42.8 %all-to-all-start = ((bf16[16,3,128,128]{3,2,1,0:T(8,128)(2,1)}), bf16[16,3,128,128]{3,2,1,0:T(8,128)(2,1)}, u32[]{:S(2)}, u32[]{:S(2)}) async-start(bf16[16,3,128,128]{3,2,1,0:T(8,128)(2,1)} %shard_map.182), calls=%async_computation | async-start | bytes 3145728 | tf_op jit(solution)/shard_map/all_to_all | solution.py:435
  10.0 7.4 %copy-start.16 = (f32[128]{0:T(128)S(1)}, f32[128]{0:T(128)}, u32[]{:S(2)}) copy-start(f32[128]{0:T(128)} %param.24) | copy-start | bytes 1540
  10.0 8.1 %copy-start.17 = (f32[128]{0:T(128)S(1)}, f32[128]{0:T(128)}, u32[]{:S(2)}) copy-start(f32[128]{0:T(128)} %param.23) | copy-start | bytes 1540
  10.0 8.8 %copy-start.2 = (f32[128,2048]{1,0:T(8,128)S(1)}, f32[128,2048]{1,0:T(8,128)}, u32[]{:S(2)}) copy-start(f32[128,2048]{1,0:T(8,128)} %one_ref.1) | copy-start | bytes 3145732
  10.1 8.8 %copy-start.3 = (f32[128,2048]{1,0:T(8,128)S(1)}, f32[128,2048]{1,0:T(8,128)}, u32[]{:S(2)}) copy-start(f32[128,2048]{1,0:T(8,128)} %two_ref.1) | copy-start | bytes 3145732
  10.1 8.8 %copy-start.4 = (bf16[256,256]{1,0:T(8,128)(2,1)S(1)}, bf16[256,256]{1,0:T(8,128)(2,1)}, u32[]{:S(2)}) copy-start(bf16[256,256]{1,0:T(8,128)(2,1)} %constant.93.clone.mat_hi) | copy-start | bytes 393220
  10.1 8.8 %copy-start.6 = (bf16[256,256]{1,0:T(8,128)(2,1)S(1)}, bf16[256,256]{1,0:T(8,128)(2,1)}, u32[]{:S(2)}) copy-start(bf16[256,256]{1,0:T(8,128)(2,1)} %constant.94.clone.mat_lo) | copy-start | bytes 393220
  10.1 8.8 %copy-start.8 = (f32[34,128]{1,0:T(8,128)S(1)}, f32[34,128]{1,0:T(8,128)}, u32[]{:S(2)}) copy-start(f32[34,128]{1,0:T(8,128)} %constant.95.clone.tw_ref.tw_scaled) | copy-start | bytes 52228
  13.5 13.7 %collective-permute-start = (bf16[2,1,128,128]{3,2,1,0:T(8,128)(2,1)}, bf16[2,1,128,128]{3,2,1,0:T(8,128)(2,1)}, u32[]{:S(2)}, u32[]{:S(2)}) collective-permute-start(bf16[2,1,128,128]{3,2,1,0:T(8,128)(2,1)} %get-tuple-element.34), channel_id=1, source_target_pairs={{0,1},{1,0},{2,3},{3,2},{4,5},{5,4},{6,7},{7,6},{8,9},{9,8},{10,11... | collective-permute-start | bytes 196616 | tf_op jit(solution)/shard_map/ppermute | solution.py:440
  13.9 16.0 %collective-permute-start.1 = (bf16[2,1,128,128]{3,2,1,0:T(8,128)(2,1)}, bf16[2,1,128,128]{3,2,1,0:T(8,128)(2,1)}, u32[]{:S(2)}, u32[]{:S(2)}) collective-permute-start(bf16[2,1,128,128]{3,2,1,0:T(8,128)(2,1)} %get-tuple-element.35), channel_id=1, source_target_pairs={{0,2},{1,3},{2,0},{3,1},{4,6},{5,7},{6,4},{7,5},{8,10},{9,11},{10,... | collective-permute-start | bytes 196616 | tf_op jit(solution)/shard_map/ppermute | solution.py:440
  15.1 17.7 %collective-permute-start.2 = (bf16[2,1,128,128]{3,2,1,0:T(8,128)(2,1)}, bf16[2,1,128,128]{3,2,1,0:T(8,128)(2,1)}, u32[]{:S(2)}, u32[]{:S(2)}) collective-permute-start(bf16[2,1,128,128]{3,2,1,0:T(8,128)(2,1)} %get-tuple-element.36), channel_id=1, source_target_pairs={{0,3},{1,2},{2,1},{3,0},{4,7},{5,6},{6,5},{7,4},{8,11},{9,10},{10,... | collective-permute-start | bytes 196616 | tf_op jit(solution)/shard_map/ppermute | solution.py:440
  15.7 22.7 %collective-permute-start.3 = (bf16[2,1,128,128]{3,2,1,0:T(8,128)(2,1)}, bf16[2,1,128,128]{3,2,1,0:T(8,128)(2,1)}, u32[]{:S(2)}, u32[]{:S(2)}) collective-permute-start(bf16[2,1,128,128]{3,2,1,0:T(8,128)(2,1)} %get-tuple-element.37), channel_id=1, source_target_pairs={{0,4},{1,5},{2,6},{3,7},{4,0},{5,1},{6,2},{7,3},{8,12},{9,13},{10,... | collective-permute-start | bytes 196616 | tf_op jit(solution)/shard_map/ppermute | solution.py:440
  15.8 24.1 %collective-permute-start.4 = (bf16[2,1,128,128]{3,2,1,0:T(8,128)(2,1)}, bf16[2,1,128,128]{3,2,1,0:T(8,128)(2,1)}, u32[]{:S(2)}, u32[]{:S(2)}) collective-permute-start(bf16[2,1,128,128]{3,2,1,0:T(8,128)(2,1)} %get-tuple-element.38), channel_id=1, source_target_pairs={{0,5},{1,4},{2,7},{3,6},{4,1},{5,0},{6,3},{7,2},{8,13},{9,12},{10,... | collective-permute-start | bytes 196616 | tf_op jit(solution)/shard_map/ppermute | solution.py:440
  27.3 14.6 %collective-permute-start.5 = (bf16[2,1,128,128]{3,2,1,0:T(8,128)(2,1)}, bf16[2,1,128,128]{3,2,1,0:T(8,128)(2,1)S(1)}, u32[]{:S(2)}, u32[]{:S(2)}) collective-permute-start(bf16[2,1,128,128]{3,2,1,0:T(8,128)(2,1)} %get-tuple-element.39), channel_id=1, source_target_pairs={{0,6},{1,7},{2,4},{3,5},{4,2},{5,3},{6,0},{7,1},{8,14},{9,15},{10,... | collective-permute-start | bytes 196616 | tf_op jit(solution)/shard_map/ppermute | solution.py:440
  29.9 14.0 %collective-permute-start.6 = (bf16[2,1,128,128]{3,2,1,0:T(8,128)(2,1)}, bf16[2,1,128,128]{3,2,1,0:T(8,128)(2,1)S(1)}, u32[]{:S(2)}, u32[]{:S(2)}) collective-permute-start(bf16[2,1,128,128]{3,2,1,0:T(8,128)(2,1)} %get-tuple-element.40), channel_id=1, source_target_pairs={{0,7},{1,6},{2,5},{3,4},{4,3},{5,2},{6,1},{7,0},{8,15},{9,14},{10,... | collective-permute-start | bytes 196616 | tf_op jit(solution)/shard_map/ppermute | solution.py:440
  44.5 12.1 %collective-permute-start.7 = (bf16[8,128,128]{2,1,0:T(8,128)(2,1)}, bf16[8,128,128]{2,1,0:T(8,128)(2,1)}, u32[]{:S(2)}, u32[]{:S(2)}) collective-permute-start(bf16[8,128,128]{2,1,0:T(8,128)(2,1)} %get-tuple-element.60), channel_id=1, source_target_pairs={{0,8},{1,9},{2,10},{3,11},{4,12},{5,13},{6,14},{7,15},{8,0},{9,1},... | collective-permute-start | bytes 786440 | tf_op jit(solution)/shard_map/ppermute | solution.py:440
  56.6 8.9 %copy-start.5 = (bf16[256,256]{1,0:T(8,128)(2,1)S(1)}, bf16[256,256]{1,0:T(8,128)(2,1)}, u32[]{:S(2)}) copy-start(bf16[256,256]{1,0:T(8,128)(2,1)} %constant.93.clone.mat_hi) | copy-start | bytes 393220
  56.6 8.9 %copy-start.7 = (bf16[256,256]{1,0:T(8,128)(2,1)S(1)}, bf16[256,256]{1,0:T(8,128)(2,1)}, u32[]{:S(2)}) copy-start(bf16[256,256]{1,0:T(8,128)(2,1)} %constant.94.clone.mat_lo) | copy-start | bytes 393220
  56.6 8.9 %copy-start.9 = (f32[34,128]{1,0:T(8,128)S(1)}, f32[34,128]{1,0:T(8,128)}, u32[]{:S(2)}) copy-start(f32[34,128]{1,0:T(8,128)} %constant.96.clone.tw_ref) | copy-start | bytes 52228
  56.6 8.9 %copy-start.12 = (bf16[16,128,128]{2,1,0:T(8,128)(2,1)S(1)}, bf16[16,128,128]{2,1,0:T(8,128)(2,1)}, u32[]{:S(2)}) copy-start(bf16[16,128,128]{2,1,0:T(8,128)(2,1)} %get-tuple-element.46.grad_ref) | copy-start | bytes 1572868
  56.7 32.7 %all-to-all-start.1 = ((bf16[16,2,128,128]{3,2,1,0:T(8,128)(2,1)}), bf16[16,2,128,128]{3,2,1,0:T(8,128)(2,1)S(1)}, u32[]{:S(2)}, u32[]{:S(2)}) async-start(bf16[16,2,128,128]{3,2,1,0:T(8,128)(2,1)} %get-tuple-element.41), calls=%async_computation.1 | async-start | bytes 2097152 | tf_op jit(solution)/shard_map/all_to_all | solution.py:435
  (4 other events, 16.2 us)

commit v2 on v1

--- a/solution.py
+++ b/solution.py
@@ -394,6 +394,39 @@
             copy.wait()
 
 
+def pairs_kernel(me_ref, gate_one, conv_one, *refs):
+    *outs, gate, conv, made, sems = refs
+    half = len(outs)
+    me = me_ref[0]
+    arrive = [pltpu.make_async_copy(ref, to, sems.at[half + i])
+              for i, (ref, to) in enumerate(((gate_one, gate), (conv_one, conv)))]
+    leave = [pltpu.make_async_copy(made.at[r], out, sems.at[r]) for r, out in enumerate(outs)]
+    for copy in arrive:
+        copy.start()
+    for copy in arrive:
+        copy.wait()
+    for r in range(half):
+        for i, index in enumerate((me ^ r, me ^ r ^ (half + half // 2))):
+            made[r, i] = product(gate[index], conv[index])
+        leave[r].start()
+    for copy in leave:
+        copy.wait()
+
+
+def join_kernel(*refs):
+    *parts, out, held, sems = refs
+    half = len(parts)
+    copies = [pltpu.make_async_copy(parts[r ^ (half // 2)].at[1], held.at[r], sems.at[r])
+              for r in range(half)]
+    for copy in copies:
+        copy.start()
+    for copy in copies:
+        copy.wait()
+    copy = pltpu.make_async_copy(held, out, sems.at[half])
+    copy.start()
+    copy.wait()
+
+
 def receive_kernel(came, conv_one, proj_grad, gate_one_grad, made, sems):
     blocks = conv_one.shape[0]
     parts = math.gcd(blocks, PARTS)
@@ -438,19 +471,6 @@
 def swap(value, step):
     count = lax.axis_size("seq")
     return lax.ppermute(value, "seq", [(j, j ^ step) for j in range(count)])
-
-
-def exchange_near(value):
-    me = lax.axis_index("seq")
-    half = value.shape[0] // 2
-    value = value.reshape((2, half) + value.shape[1:])
-    mine = me // half
-    value = jnp.concatenate(
-        [lax.dynamic_index_in_dim(value, mine, 0), lax.dynamic_index_in_dim(value, 1 - mine, 0)])
-    parts = [lax.dynamic_index_in_dim(value, (me % half) ^ r, 1) for r in range(half)]
-    parts = lax.optimization_barrier(tuple(parts))
-    came = [parts[0]] + [swap(parts[r], r) for r in range(1, half)]
-    return ([part[0] for part in came], jnp.concatenate([part[1] for part in came]))
 
 
 def local(
@@ -496,13 +516,25 @@
         send_kernel, [triple], [(shape, BF16)] * 5, 3 * pair.size, 7 * pair.size,
         *(a.reshape(shape) for a in (out_grad, gate_two, gate_one, value)),
         far=range(4), far_out=True, copies=7 * parts, limit=WHOLE)[0])
-    near, far = exchange_near(product(gate_one, conv_one).reshape(shape))
+    half = blocks // 2
+    half_shape = (half, channels, width)
+    here = me[None].astype(jnp.int32)
+    parts_of = call(
+        pairs_kernel, [struct(2, channels, width, dtype=BF16)] * half,
+        [(shape, BF16), (shape, BF16), ((half, 2, channels, width), BF16)],
+        pair.size, 2 * pair.size, here, gate_one.reshape(shape), conv_one.reshape(shape),
+        far=(1, 2), far_out=True, copies=half + 2, limit=WHOLE)
+    came = [parts_of[0]] + [swap(parts_of[r], r) for r in range(1, half)]
+    far = call(join_kernel, [struct(*half_shape, dtype=BF16)], [(half_shape, BF16)],
+               pair.size, pair.size, *came, far=range(half), far_out=True, copies=half + 1,
+               limit=WHOLE)[0]
+    near = [part[:1] for part in came]
     h_one, h_two = call(
         functools.partial(spectrum_kernel, blocks, width),
         [spec, spec], halves, 2 * work, 4 * size,
         filter_one, filter_two, mat_hi, mat_lo, tw_scaled)
     gate_two_grad = product(out_grad, conv_two)
-    far = swap(far, blocks // 2)
+    far = swap(far, blocks // 2 + blocks // 4)
     first, h_one, h_two, gate_two_grad = lax.optimization_barrier(
         (first, h_one, h_two, gate_two_grad))
     grads, cg_one = call(
@@ -513,14 +545,14 @@
         4 * work, 8 * size,
         first, h_two, h_one, skip_two[:, None], skip_one[:, None], taps, mat_hi, mat_lo, tw,
         far=(0, 1, 2), far_out=True, copies=6 * math.gcd(groups, PARTS), limit=WHOLE)
-    grads, far = lax.optimization_barrier((grads, far))
+    cg_one, far = lax.optimization_barrier((cg_one, far))
     inner = jnp.concatenate(near + [far])
     third = exchange(grads)
     filter_one_grad, filter_two_grad = call(
         functools.partial(filter_kernel, blocks, width),
         [struct(channels, length), struct(channels, length)],
         halves * 2 + [back], 6 * work, 8 * size,
-        me[None].astype(jnp.int32), first, inner, cg_one, mat_hi, mat_lo, tw, tw_scaled)
+        here, first, inner, cg_one, mat_hi, mat_lo, tw, tw_scaled)
     proj_grad, gate_one_grad = call(
         receive_kernel, [one, one], [(shape, BF16)], pair.size, 6 * pair.size,
         third, conv_one.reshape(shape), far_out=True, copies=parts + 1)

time: 91.3 us -> 89.7 us (0.982)
  Pallas kernels: 30.2 us -> 34.1 us
  local copies, waits for them, and re-layouts: 16 us -> 12.8 us
  starting transfers between devices: 21.2 us -> 19.5 us
  other arithmetic: 3.28 us -> 1.97 us
    ppermute x8, waiting for transfers between devices: 6.33 us -> 11.6 us  [swap(): return lax.ppermute(value, 'seq', [(j, j ^ step) for j in range(count)])]
    all_to_all x2, waiting for transfers between devices: 12.5 us -> 7.62 us  [exchange(): return lax.all_to_all(value, 'seq', split_axis=0, concat_axis=0, tiled=True)]
    all_to_all x2, starting transfers between devices: 14.6 us -> 10.6 us  [exchange(): return lax.all_to_all(value, 'seq', split_axis=0, concat_axis=0, tiled=True)]
    pallas_call x5 -> x7, Pallas kernels: 30.2 us -> 34.1 us  [call(): pl.pallas_call(kernel, out_shape=out_shape, in_specs=[smem if a.dtype ==...]
    ppermute x8, starting transfers between devices: 6.58 us -> 8.91 us  [swap(): return lax.ppermute(value, 'seq', [(j, j ^ step) for j in range(count)])]
    concatenate x2 -> x0, other arithmetic: 1.42 us -> none  [exchange_near(): jnp.concatenate([lax.dynamic_index_in_dim(value, mine, 0), lax.dynamic_in...]
    unnamed x45 -> x53, local copies, waits for them, and re-layouts: 12.5 us -> 11.3 us
    dynamic_slice x1 -> x0, local copies, waits for them, and re-layouts: 1.07 us -> none  [exchange_near(): lax.dynamic_index_in_dim(value, 1 - mine, 0)]
  transfers between devices with their start and end apart: 10 -> 10, of which waited for: 6 -> 5; matrix products, arithmetic and copies ran while one was open for 18% -> 10% of each run, Pallas kernels for 29% -> 34%
where the time goes in v2:
time: 89.7 us; the launch traced here: 88.7 us
  Pallas kernels  34.1 us (38%)
  starting transfers between devices  19.5 us (22%)
  waiting for transfers between devices  19.2 us (21%)
  local copies, waits for them, and re-layouts  12.8 us (14%)
  other arithmetic  1.97 us (2%)
  between operations  1.04 us (1%)
    pallas_call x7, Pallas kernels, call(): pl.pallas_call(kernel, out_shape=out_shape, in_specs=[smem if a.dtype ==...  34.1 us
    ppermute x8, waiting for transfers between devices, swap(): return lax.ppermute(value, 'seq', [(j, j ^ step) for j in range(count)])  11.6 us
    unnamed x53, local copies, waits for them, and re-layouts  11.3 us
    all_to_all x2, starting transfers between devices, exchange(): return lax.all_to_all(value, 'seq', split_axis=0, concat_axis=0, tiled=True)  10.6 us
    ppermute x8, starting transfers between devices, swap(): return lax.ppermute(value, 'seq', [(j, j ^ step) for j in range(count)])  8.91 us
    all_to_all x2, waiting for transfers between devices, exchange(): return lax.all_to_all(value, 'seq', split_axis=0, concat_axis=0, tiled=True)  7.62 us
    convert_element_type x1, other arithmetic, product(): return (a.astype(F32) * b.astype(F32)).astype(BF16)  1.97 us
  transfers between devices with their start and end apart: 10, of which 5 were waited for; matrix products, arithmetic and copies ran while one was open for 10% of the time, Pallas kernels for 34%

profile of v2, /device:TPU:9, one launch (start us, length us, event | category | flops | bytes accessed | tf_op | source)
XLA Modules:
  0.0 88.7 jit_solution(8430448455113173461)
XLA Ops:
  0.6 2.6 %shard_map.182 = bf16[16,3,128,128]{3,2,1,0:T(8,128)(2,1)} custom-call(bf16[16,128,128]{2,1,0:T(8,128)(2,1)} %bitcast.12, bf16[16,128,128]{2,1,0:T(8,128)(2,1)} %bitcast.15, bf16[16,128,128]{2,1,0:T(8,128)(2,1)} %bitcast.13, bf16[16,128,128]{2,1,0:T(8,128)(2,1)} %bitcast.16), custom_call_target="tpu_custom_call" | custom-call | flops 1572864 | bytes 3670016 | tf_op jit(solution)/shard_map/pallas_call | solution.py:454
  3.3 6.8 %all-to-all-start = ((bf16[16,3,128,128]{3,2,1,0:T(8,128)(2,1)}), bf16[16,3,128,128]{3,2,1,0:T(8,128)(2,1)}, u32[]{:S(2)}, u32[]{:S(2)}) async-start(bf16[16,3,128,128]{3,2,1,0:T(8,128)(2,1)} %shard_map.182), calls=%async_computation | async-start | bytes 3145728 | tf_op jit(solution)/shard_map/all_to_all | solution.py:468
  10.0 2.1 %shard_map.186 = (bf16[2,128,128]{2,1,0:T(8,128)(2,1)}, bf16[2,128,128]{2,1,0:T(8,128)(2,1)}, bf16[2,128,128]{2,1,0:T(8,128)(2,1)}, bf16[2,128,128]{2,1,0:T(8,12...) custom-call(s32[1]{0:T(128)} %bitcast.9.me_ref, ...), custom_call_target="tpu_custom_call" | custom-call | flops 524288 | bytes 1048576 | tf_op jit(solution)/shard_map/pallas_call | solution.py:454
  12.5 1.2 %collective-permute-start.1 = (bf16[2,128,128]{2,1,0:T(8,128)(2,1)}, bf16[2,128,128]{2,1,0:T(8,128)(2,1)}, u32[]{:S(2)}, u32[]{:S(2)}) collective-permute-start(bf16[2,128,128]{2,1,0:T(8,128)(2,1)} %get-tuple-element.38), channel_id=1, source_target_pairs={{0,2},{1,3},{2,0},{3,1},{4,6},{5,7},{6,4},{7,5},{8,10},{9,11},{10,... | collective-permute-start | bytes 196616 | tf_op jit(solution)/shard_map/ppermute | solution.py:473
  14.4 1.6 %collective-permute-start.4 = (bf16[2,128,128]{2,1,0:T(8,128)(2,1)}, bf16[2,128,128]{2,1,0:T(8,128)(2,1)}, u32[]{:S(2)}, u32[]{:S(2)}) collective-permute-start(bf16[2,128,128]{2,1,0:T(8,128)(2,1)} %get-tuple-element.41), channel_id=1, source_target_pairs={{0,5},{1,4},{2,7},{3,6},{4,1},{5,0},{6,3},{7,2},{8,13},{9,12},{10,... | collective-permute-start | bytes 196616 | tf_op jit(solution)/shard_map/ppermute | solution.py:473
  16.8 2.0 %multiply_convert_fusion = bf16[2048,128]{1,0:T(8,128)(2,1)} fusion(bf16[2048,128]{1,0:T(8,128)(2,1)} %param.19, bf16[2048,128]{1,0:T(8,128)(2,1)S(1)} %copy-done.13), kind=kLoop, calls=%fused_computation | loop fusion | flops 1048576 | bytes 1572864 | tf_op jit(solution)/shard_map/convert_element_type | solution.py:364
  18.8 1.2 %copy-done.2 = f32[128,2048]{1,0:T(8,128)S(1)} copy-done((f32[128,2048]{1,0:T(8,128)S(1)}, f32[128,2048]{1,0:T(8,128)}, u32[]{:S(2)}) %copy-start.2) | copy-done | bytes 1048600
  20.0 1.2 %copy-done.3 = f32[128,2048]{1,0:T(8,128)S(1)} copy-done((f32[128,2048]{1,0:T(8,128)S(1)}, f32[128,2048]{1,0:T(8,128)}, u32[]{:S(2)}) %copy-start.3) | copy-done | bytes 1048600
  21.2 3.3 %shard_map.183 = (f32[8,272,256]{2,1,0:T(8,128)S(1)}, f32[8,272,256]{2,1,0:T(8,128)S(1)}) custom-call(f32[128,2048]{1,0:T(8,128)S(1)} %copy-done.2, f32[128,2048]{1,0:T(8,128)S(1)} %copy-done.3, bf16[256,256]{1,0:T(8,128)(2,1)S(1)} %copy-done.4, bf16[256,256]{1,0:T(8,128)(2,1)S(1)} %copy-done.6, f32[34,128]{1,0:T(8,128)S(1)} %copy-done.8), custom_call_target="tpu_custom_call" | custom-call | flops 1711276032 | bytes 8912896 | tf_op jit(solution)/shard_map/pallas_call | solution.py:454
  24.6 1.4 %copy-done.10 = f32[8,272,256]{2,1,0:T(8,128)} copy-done((f32[8,272,256]{2,1,0:T(8,128)}, f32[8,272,256]{2,1,0:T(8,128)S(1)}, u32[]{:S(2)}) %copy-start.10) | copy-done | bytes 2228248
  26.0 1.4 %copy-done.11 = f32[8,272,256]{2,1,0:T(8,128)} copy-done((f32[8,272,256]{2,1,0:T(8,128)}, f32[8,272,256]{2,1,0:T(8,128)S(1)}, u32[]{:S(2)}) %copy-start.11) | copy-done | bytes 2228248
  28.9 1.2 %collective-permute-start.5 = (bf16[2,128,128]{2,1,0:T(8,128)(2,1)S(1)}, bf16[2,128,128]{2,1,0:T(8,128)(2,1)S(1)}, u32[]{:S(2)}, u32[]{:S(2)}) collective-permute-start(bf16[2,128,128]{2,1,0:T(8,128)(2,1)S(1)} %copy-done.21), channel_id=1, source_target_pairs={{0,6},{1,7},{2,4},{3,5},{4,2},{5,3},{6,0},{7,1},{8,14},{9,15},{10,... | collective-permute-start | bytes 196616 | tf_op jit(solution)/shard_map/ppermute | solution.py:473
  30.0 1.5 %collective-permute-start.6 = (bf16[2,128,128]{2,1,0:T(8,128)(2,1)S(1)}, bf16[2,128,128]{2,1,0:T(8,128)(2,1)S(1)}, u32[]{:S(2)}, u32[]{:S(2)}) collective-permute-start(bf16[2,128,128]{2,1,0:T(8,128)(2,1)S(1)} %copy-done.20), channel_id=1, source_target_pairs={{0,7},{1,6},{2,5},{3,4},{4,3},{5,2},{6,1},{7,0},{8,15},{9,14},{10,... | collective-permute-start | bytes 196616 | tf_op jit(solution)/shard_map/ppermute | solution.py:473
  32.3 6.1 %collective-permute-done.3.refs_4_ = bf16[2,128,128]{2,1,0:T(8,128)(2,1)} collective-permute-done((bf16[2,128,128]{2,1,0:T(8,128)(2,1)}, bf16[2,128,128]{2,1,0:T(8,128)(2,1)}, u32[]{:S(2)}, u32[]{:S(2)}) %collective-permute-start.3) | collective-permute-done | bytes 65568 | tf_op jit(solution)/shard_map/ppermute | solution.py:473
  38.4 1.5 %collective-permute-done.4.refs_5_ = bf16[2,128,128]{2,1,0:T(8,128)(2,1)} collective-permute-done((bf16[2,128,128]{2,1,0:T(8,128)(2,1)}, bf16[2,128,128]{2,1,0:T(8,128)(2,1)}, u32[]{:S(2)}, u32[]{:S(2)}) %collective-permute-start.4) | collective-permute-done | bytes 65568 | tf_op jit(solution)/shard_map/ppermute | solution.py:473
  39.9 2.0 %collective-permute-done.5.refs_6_ = bf16[2,128,128]{2,1,0:T(8,128)(2,1)S(1)} collective-permute-done((bf16[2,128,128]{2,1,0:T(8,128)(2,1)S(1)}, bf16[2,128,128]{2,1,0:T(8,128)(2,1)S(1)}, u32[]{:S(2)}, u32[]{:S(2)}) %collective-permute-start.5) | collective-permute-done | bytes 65568 | tf_op jit(solution)/shard_map/ppermute | solution.py:473
  41.9 2.1 %collective-permute-done.6.refs_7_ = bf16[2,128,128]{2,1,0:T(8,128)(2,1)S(1)} collective-permute-done((bf16[2,128,128]{2,1,0:T(8,128)(2,1)S(1)}, bf16[2,128,128]{2,1,0:T(8,128)(2,1)S(1)}, u32[]{:S(2)}, u32[]{:S(2)}) %collective-permute-start.6) | collective-permute-done | bytes 65568 | tf_op jit(solution)/shard_map/ppermute | solution.py:473
  44.6 1.6 %shard_map.187 = bf16[8,128,128]{2,1,0:T(8,128)(2,1)} custom-call(bf16[2,128,128]{2,1,0:T(8,128)(2,1)} %get-tuple-element.36.refs_0_, bf16[2,128,128]{2,1,0:T(8,128)(2,1)} %collective-permute-done.refs_1_, bf16[2,128,128]{2,1,0:T(8,128)(2,1)} %collective-permute-done.1.refs_2_, bf16[2,128,128]{2,1,0:T(8,128)(2,1)} %collective-permute-done.2.refs_3_, ...), custom_call_target="tpu_custom_call" | custom-call | flops 524288 | bytes 524288 | tf_op jit(solution)/shard_map/pallas_call | solution.py:454
  46.2 2.3 %collective-permute-start.7 = (bf16[8,128,128]{2,1,0:T(8,128)(2,1)}, bf16[8,128,128]{2,1,0:T(8,128)(2,1)S(1)}, u32[]{:S(2)}, u32[]{:S(2)}) collective-permute-start(bf16[8,128,128]{2,1,0:T(8,128)(2,1)} %shard_map.187), channel_id=1, source_target_pairs={{0,12},{1,13},{2,14},{3,15},{4,8},{5,9},{6,10},{7,11},{8,4},{9,5},... | collective-permute-start | bytes 786440 | tf_op jit(solution)/shard_map/ppermute | solution.py:473
  48.5 10.5 %shard_map.184 = (bf16[16,2,128,128]{3,2,1,0:T(8,128)(2,1)}, bf16[16,128,128]{2,1,0:T(8,128)(2,1)}) custom-call(bf16[16,3,128,128]{3,2,1,0:T(8,128)(2,1)} %all-to-all-done.sent.in_ref, f32[8,272,256]{2,1,0:T(8,128)} %copy-done.11, f32[8,272,256]{2,1,0:T(8,128)} %copy-done.10, f32[128,1]{1,0:T(8,128)} %copy.21.skip_two, f32[128,1]{1,0:T(8,128)} %copy.22.skip_one, ...), custom_call_target="tpu_custom_call" | custom-call | flops 3422552064 | bytes 17825792 | tf_op jit(solution)/shard_map/pallas_call | solution.py:454
  59.1 3.9 %all-to-all-start.1 = ((bf16[16,2,128,128]{3,2,1,0:T(8,128)(2,1)}), bf16[16,2,128,128]{3,2,1,0:T(8,128)(2,1)S(1)}, u32[]{:S(2)}, u32[]{:S(2)}) async-start(bf16[16,2,128,128]{3,2,1,0:T(8,128)(2,1)} %get-tuple-element.32), calls=%async_computation.1 | async-start | bytes 2097152 | tf_op jit(solution)/shard_map/all_to_all | solution.py:468
  67.0 13.0 %shard_map.188 = (f32[128,2048]{1,0:T(8,128)}, f32[128,2048]{1,0:T(8,128)}) custom-call(s32[1]{0:T(128)} %bitcast.9.me_ref, bf16[16,3,128,128]{3,2,1,0:T(8,128)(2,1)} %all-to-all-done.sent.in_ref, bf16[16,128,128]{2,1,0:T(8,128)(2,1)S(1)} %constant_dynamic-update-slice_fusion.inner_ref, bf16[16,128,128]{2,1,0:T(8,128)(2,1)S(1)} %copy-done.12, ...), custom_call_target="tpu_custom_call" | custom-call | flops 5133828096 | bytes 17825792 | tf_op jit(solution)/shard_map/pallas_call | solution.py:454
  80.0 7.6 %all-to-all-done.1.came = bf16[16,2,128,128]{3,2,1,0:T(8,128)(2,1)S(1)} async-done(((bf16[16,2,128,128]{3,2,1,0:T(8,128)(2,1)}), bf16[16,2,128,128]{3,2,1,0:T(8,128)(2,1)S(1)}, u32[]{:S(2)}, u32[]{:S(2)}) %all-to-all-start.1) | async-done | bytes 1048608 | tf_op jit(solution)/shard_map/all_to_all | solution.py:468
  87.6 1.0 %shard_map.185 = (bf16[16,128,128]{2,1,0:T(8,128)(2,1)}, bf16[16,128,128]{2,1,0:T(8,128)(2,1)}) custom-call(bf16[16,2,128,128]{3,2,1,0:T(8,128)(2,1)S(1)} %all-to-all-done.1.came, bf16[16,128,128]{2,1,0:T(8,128)(2,1)S(1)} %bitcast.11), custom_call_target="tpu_custom_call" | custom-call | flops 524288 | bytes 3145728 | tf_op jit(solution)/shard_map/pallas_call | solution.py:454
  (61 shorter events, 8.7 us)
Async XLA Ops:
  0.6 30.9 %copy-start = (f32[2048,3]{0,1:T(4,128)S(1)}, f32[2048,3]{0,1:T(4,128)}, u32[]{:S(2)}) copy-start(f32[2048,3]{0,1:T(4,128)} %param.25) | copy-start | bytes 73732
  3.2 13.6 %copy-start.13 = (bf16[2048,128]{1,0:T(8,128)(2,1)S(1)}, bf16[2048,128]{1,0:T(8,128)(2,1)}, u32[]{:S(2)}) copy-start(bf16[2048,128]{1,0:T(8,128)(2,1)} %param.15) | copy-start | bytes 1572868
  3.2 15.5 %copy-start.4 = (bf16[256,256]{1,0:T(8,128)(2,1)S(1)}, bf16[256,256]{1,0:T(8,128)(2,1)}, u32[]{:S(2)}) copy-start(bf16[256,256]{1,0:T(8,128)(2,1)} %constant.18.clone.mat_hi) | copy-start | bytes 393220
  3.2 15.5 %copy-start.6 = (bf16[256,256]{1,0:T(8,128)(2,1)S(1)}, bf16[256,256]{1,0:T(8,128)(2,1)}, u32[]{:S(2)}) copy-start(bf16[256,256]{1,0:T(8,128)(2,1)} %constant.19.clone.mat_lo) | copy-start | bytes 393220
  3.3 15.5 %copy-start.8 = (f32[34,128]{1,0:T(8,128)S(1)}, f32[34,128]{1,0:T(8,128)}, u32[]{:S(2)}) copy-start(f32[34,128]{1,0:T(8,128)} %constant.20.clone.tw_ref.tw_scaled) | copy-start | bytes 52228
  3.3 45.2 %all-to-all-start = ((bf16[16,3,128,128]{3,2,1,0:T(8,128)(2,1)}), bf16[16,3,128,128]{3,2,1,0:T(8,128)(2,1)}, u32[]{:S(2)}, u32[]{:S(2)}) async-start(bf16[16,3,128,128]{3,2,1,0:T(8,128)(2,1)} %shard_map.182), calls=%async_computation | async-start | bytes 3145728 | tf_op jit(solution)/shard_map/all_to_all | solution.py:468
  12.1 16.7 %collective-permute-start = (bf16[2,128,128]{2,1,0:T(8,128)(2,1)}, bf16[2,128,128]{2,1,0:T(8,128)(2,1)}, u32[]{:S(2)}, u32[]{:S(2)}) collective-permute-start(bf16[2,128,128]{2,1,0:T(8,128)(2,1)} %get-tuple-element.37), channel_id=1, source_target_pairs={{0,1},{1,0},{2,3},{3,2},{4,5},{5,4},{6,7},{7,6},{8,9},{9,8},{10,11... | collective-permute-start | bytes 196616 | tf_op jit(solution)/shard_map/ppermute | solution.py:473
  12.5 17.5 %collective-permute-start.1 = (bf16[2,128,128]{2,1,0:T(8,128)(2,1)}, bf16[2,128,128]{2,1,0:T(8,128)(2,1)}, u32[]{:S(2)}, u32[]{:S(2)}) collective-permute-start(bf16[2,128,128]{2,1,0:T(8,128)(2,1)} %get-tuple-element.38), channel_id=1, source_target_pairs={{0,2},{1,3},{2,0},{3,1},{4,6},{5,7},{6,4},{7,5},{8,10},{9,11},{10,... | collective-permute-start | bytes 196616 | tf_op jit(solution)/shard_map/ppermute | solution.py:473
  13.7 18.6 %collective-permute-start.2 = (bf16[2,128,128]{2,1,0:T(8,128)(2,1)}, bf16[2,128,128]{2,1,0:T(8,128)(2,1)}, u32[]{:S(2)}, u32[]{:S(2)}) collective-permute-start(bf16[2,128,128]{2,1,0:T(8,128)(2,1)} %get-tuple-element.39), channel_id=1, source_target_pairs={{0,3},{1,2},{2,1},{3,0},{4,7},{5,6},{6,5},{7,4},{8,11},{9,10},{10,... | collective-permute-start | bytes 196616 | tf_op jit(solution)/shard_map/ppermute | solution.py:473
  14.3 24.1 %collective-permute-start.3 = (bf16[2,128,128]{2,1,0:T(8,128)(2,1)}, bf16[2,128,128]{2,1,0:T(8,128)(2,1)}, u32[]{:S(2)}, u32[]{:S(2)}) collective-permute-start(bf16[2,128,128]{2,1,0:T(8,128)(2,1)} %get-tuple-element.40), channel_id=1, source_target_pairs={{0,4},{1,5},{2,6},{3,7},{4,0},{5,1},{6,2},{7,3},{8,12},{9,13},{10,... | collective-permute-start | bytes 196616 | tf_op jit(solution)/shard_map/ppermute | solution.py:473
  14.4 25.5 %collective-permute-start.4 = (bf16[2,128,128]{2,1,0:T(8,128)(2,1)}, bf16[2,128,128]{2,1,0:T(8,128)(2,1)}, u32[]{:S(2)}, u32[]{:S(2)}) collective-permute-start(bf16[2,128,128]{2,1,0:T(8,128)(2,1)} %get-tuple-element.41), channel_id=1, source_target_pairs={{0,5},{1,4},{2,7},{3,6},{4,1},{5,0},{6,3},{7,2},{8,13},{9,12},{10,... | collective-permute-start | bytes 196616 | tf_op jit(solution)/shard_map/ppermute | solution.py:473
  21.2 7.6 %copy-start.21 = (bf16[2,128,128]{2,1,0:T(8,128)(2,1)S(1)}, bf16[2,128,128]{2,1,0:T(8,128)(2,1)}, u32[]{:S(2)}) copy-start(bf16[2,128,128]{2,1,0:T(8,128)(2,1)} %get-tuple-element.42) | copy-start | bytes 196612
  21.2 8.8 %copy-start.20 = (bf16[2,128,128]{2,1,0:T(8,128)(2,1)S(1)}, bf16[2,128,128]{2,1,0:T(8,128)(2,1)}, u32[]{:S(2)}) copy-start(bf16[2,128,128]{2,1,0:T(8,128)(2,1)} %get-tuple-element.43) | copy-start | bytes 196612
  28.9 13.0 %collective-permute-start.5 = (bf16[2,128,128]{2,1,0:T(8,128)(2,1)S(1)}, bf16[2,128,128]{2,1,0:T(8,128)(2,1)S(1)}, u32[]{:S(2)}, u32[]{:S(2)}) collective-permute-start(bf16[2,128,128]{2,1,0:T(8,128)(2,1)S(1)} %copy-done.21), channel_id=1, source_target_pairs={{0,6},{1,7},{2,4},{3,5},{4,2},{5,3},{6,0},{7,1},{8,14},{9,15},{10,... | collective-permute-start | bytes 196616 | tf_op jit(solution)/shard_map/ppermute | solution.py:473
  30.0 13.9 %collective-permute-start.6 = (bf16[2,128,128]{2,1,0:T(8,128)(2,1)S(1)}, bf16[2,128,128]{2,1,0:T(8,128)(2,1)S(1)}, u32[]{:S(2)}, u32[]{:S(2)}) collective-permute-start(bf16[2,128,128]{2,1,0:T(8,128)(2,1)S(1)} %copy-done.20), channel_id=1, source_target_pairs={{0,7},{1,6},{2,5},{3,4},{4,3},{5,2},{6,1},{7,0},{8,15},{9,14},{10,... | collective-permute-start | bytes 196616 | tf_op jit(solution)/shard_map/ppermute | solution.py:473
  46.2 20.7 %collective-permute-start.7 = (bf16[8,128,128]{2,1,0:T(8,128)(2,1)}, bf16[8,128,128]{2,1,0:T(8,128)(2,1)S(1)}, u32[]{:S(2)}, u32[]{:S(2)}) collective-permute-start(bf16[8,128,128]{2,1,0:T(8,128)(2,1)} %shard_map.187), channel_id=1, source_target_pairs={{0,12},{1,13},{2,14},{3,15},{4,8},{5,9},{6,10},{7,11},{8,4},{9,5},... | collective-permute-start | bytes 786440 | tf_op jit(solution)/shard_map/ppermute | solution.py:473
  59.1 7.8 %copy-start.15 = (bf16[2,128,128]{2,1,0:T(8,128)(2,1)S(1)}, bf16[2,128,128]{2,1,0:T(8,128)(2,1)}, u32[]{:S(2)}) copy-start(bf16[2,128,128]{2,1,0:T(8,128)(2,1)} %copy-done.14) | copy-start | bytes 196612
  59.1 7.8 %copy-start.17 = (bf16[2,128,128]{2,1,0:T(8,128)(2,1)S(1)}, bf16[2,128,128]{2,1,0:T(8,128)(2,1)}, u32[]{:S(2)}) copy-start(bf16[2,128,128]{2,1,0:T(8,128)(2,1)} %copy-done.16) | copy-start | bytes 196612
  59.1 7.9 %copy-start.5 = (bf16[256,256]{1,0:T(8,128)(2,1)S(1)}, bf16[256,256]{1,0:T(8,128)(2,1)}, u32[]{:S(2)}) copy-start(bf16[256,256]{1,0:T(8,128)(2,1)} %constant.18.clone.mat_hi) | copy-start | bytes 393220
  59.1 7.9 %copy-start.7 = (bf16[256,256]{1,0:T(8,128)(2,1)S(1)}, bf16[256,256]{1,0:T(8,128)(2,1)}, u32[]{:S(2)}) copy-start(bf16[256,256]{1,0:T(8,128)(2,1)} %constant.19.clone.mat_lo) | copy-start | bytes 393220
  59.1 7.9 %copy-start.9 = (f32[34,128]{1,0:T(8,128)S(1)}, f32[34,128]{1,0:T(8,128)}, u32[]{:S(2)}) copy-start(f32[34,128]{1,0:T(8,128)} %constant.21.clone.tw_ref) | copy-start | bytes 52228
  59.1 7.9 %copy-start.12 = (bf16[16,128,128]{2,1,0:T(8,128)(2,1)S(1)}, bf16[16,128,128]{2,1,0:T(8,128)(2,1)}, u32[]{:S(2)}) copy-start(bf16[16,128,128]{2,1,0:T(8,128)(2,1)} %get-tuple-element.46.grad_ref) | copy-start | bytes 1572868
  59.1 28.4 %all-to-all-start.1 = ((bf16[16,2,128,128]{3,2,1,0:T(8,128)(2,1)}), bf16[16,2,128,128]{3,2,1,0:T(8,128)(2,1)S(1)}, u32[]{:S(2)}, u32[]{:S(2)}) async-start(bf16[16,2,128,128]{3,2,1,0:T(8,128)(2,1)} %get-tuple-element.32), calls=%async_computation.1 | async-start | bytes 2097152 | tf_op jit(solution)/shard_map/all_to_all | solution.py:468
  67.0 20.6 %copy-start.1 = (bf16[2048,128]{1,0:T(8,128)(2,1)S(1)}, bf16[2048,128]{1,0:T(8,128)(2,1)}, u32[]{:S(2)}) copy-start(bf16[2048,128]{1,0:T(8,128)(2,1)} %param.18) | copy-start | bytes 1572868
  (8 other events, 20.9 us)
